TPU v7x, 512 devices: a whole 4x4x16 slice. The times are simulated.
512 devices in a mesh: pts: 128 (over z, y, core), grp: 4 (over x).
Axes of the slice: x: 4, y: 4, z: 16, core: 2. Of those that a mesh axis runs over, the one named last changes fastest.
Arguments:
- feats4: bfloat16 [262144, 256], P(('pts', 'grp')), may hold values from -6 to 6
- order4: int32 [262144], P(('pts', 'grp')), may hold values from 0 to 262143, as said below
- gain4: float32 [256], replicated, may hold values from 0.25 to 1.75
- qkv4: bfloat16 [3, 256, 256], replicated
- proj4: bfloat16 [256, 256], replicated, may hold values from -0.375 to 0.375
- pool_weight: bfloat16 [256, 512], replicated, may hold values from -0.375 to 0.375
- child5: int32 [65536, 8], P('pts'), may hold values from 0 to 262143, as said below
- mask5: int32 [65536, 8], P('pts'), may hold values from 0 to 1, as said below
- order5: int32 [65536], P('pts'), may hold values from 0 to 65535, as said below
- gain5: float32 [512], replicated, may hold values from 0.25 to 1.75
- qkv5: bfloat16 [3, 512, 512], P(None, None, 'grp')
- proj5: bfloat16 [512, 512], P('grp'), may hold values from -0.25 to 0.25
Outputs:
- fine_out: bfloat16 [262144, 256], P(('pts', 'grp'))
- coarse_out: bfloat16 [65536, 512], P('pts', 'grp')
Inputs may be any that keep to these rules, and one draw needn't show every extreme that they name: `order4`: A permutation of the 262144 section-4 rows; the 512 curve positions of one device take exactly 1 row from the owner rows of each device. Section-5 point i has c children, c from 1 to 8: the consecutive section-4 curve positions child5[i, 0] to child5[i, 0] + c - 1 in slots 0 to c - 1; later slots hold arbitrary section-4 curve positions of the same index of pts. The children of the 512 points of one index of pts are the 2048 section-4 curve positions of that index, each once, in the order of the points. Every index of pts has a point with 8 children. `mask5`: 1 exactly on the slots that hold children. `order5`: A permutation of the 65536 pooled rows; the 512 curve positions of one index of pts take exactly 4 rows from the pooled rows of each index.
All inputs are finite; a program needn't handle non-finite values.
Results may differ from a plain program's by a relative error of at most 0.022.
The roundings to bfloat16 on the way count: a program that leaves them out, or rounds other values in their place, can miss the bound.
Values may be sent and summed in bfloat16 or wider, within the bound.
No kernel may reach another device: no remote copies, remote signals or barrier semaphores. Data moves between devices by JAX's collectives and lax.ppermute only.
A program may use at most 64 MiB of HBM per device.

v0:
```python
import math

import jax
import jax.numpy as jnp
from jax import lax
from jax.sharding import PartitionSpec as P

C4 = 256
H4 = 16
C5 = 512
H5 = 32


epsilon = 1e-05


def partner(block, axis, bit):
    count = lax.axis_size(axis)
    route = []
    for low in range(count):
        high = low | 1 << bit
        if high != low and high < count:
            route += [(low, high), (high, low)]
    return lax.ppermute(block, axis, route)


def layer_norm(rows_in, norm_gain):
    values = rows_in.astype(jnp.float32)
    center = values - jnp.mean(values, axis=-1, keepdims=True)
    spread = jnp.mean(center * center, axis=-1, keepdims=True)
    return (center * lax.rsqrt(spread + epsilon) * norm_gain).astype(jnp.bfloat16)


def one_head(queries, key_rows, value_rows, scaling):
    scores = (
        jnp.einsum("qd,kd->qk", queries, key_rows, preferred_element_type=jnp.float32) * scaling
    )
    row_max = jnp.max(scores, axis=-1, keepdims=True)
    weights = jnp.exp(scores - row_max)
    probabilities = (weights / jnp.sum(weights, axis=-1, keepdims=True)).astype(jnp.bfloat16)
    return jnp.dot(probabilities, value_rows, preferred_element_type=jnp.float32).astype(
        jnp.bfloat16
    )


def patch_attention(queries, key_rows, value_rows, head_size):
    row_count = queries.shape[0]
    key_count = key_rows.shape[0]
    head_count = queries.shape[1] // head_size
    split_query = queries.reshape(row_count, head_count, head_size).transpose(1, 0, 2)
    split_key = key_rows.reshape(key_count, head_count, head_size).transpose(1, 0, 2)
    split_value = value_rows.reshape(key_count, head_count, head_size).transpose(1, 0, 2)
    scaling = 1.0 / math.sqrt(head_size)

    def per_head(triple):
        return one_head(triple[0], triple[1], triple[2], scaling)

    mixed_heads = lax.map(per_head, (split_query, split_key, split_value))
    return mixed_heads.transpose(1, 0, 2).reshape(row_count, head_count * head_size)


def project_three(normed, weights):
    return jnp.einsum("rc,tcd->trd", normed, weights, preferred_element_type=jnp.float32).astype(
        jnp.bfloat16
    )


def local(
    feats4, order4, gain4, qkv4, proj4, pool_weight, child5, mask5, order5, gain5, qkv5, proj5
):
    fine_count = feats4.shape[0]
    fine_width = feats4.shape[1]
    pts_count = lax.axis_size("pts")
    grp_count = lax.axis_size("grp")
    pts_index = lax.axis_index("pts")
    grp_index = lax.axis_index("grp")
    per_peer = fine_count // (pts_count * grp_count)
    owner_flat = order4 // fine_count
    sorted_slots = jnp.argsort(owner_flat, stable=True)
    wanted = (order4[sorted_slots] - owner_flat[sorted_slots] * fine_count).reshape(
        pts_count, grp_count, per_peer
    )
    incoming = lax.all_to_all(
        lax.all_to_all(wanted, "pts", split_axis=0, concat_axis=0, tiled=True),
        "grp",
        split_axis=1,
        concat_axis=1,
        tiled=True,
    )
    outgoing = feats4[incoming]
    returned = lax.all_to_all(
        lax.all_to_all(outgoing, "pts", split_axis=0, concat_axis=0, tiled=True),
        "grp",
        split_axis=1,
        concat_axis=1,
        tiled=True,
    )
    arrived = returned.reshape(fine_count, fine_width)
    curve_rows = arrived[jnp.argsort(sorted_slots)]
    normed4 = layer_norm(curve_rows, gain4)
    projected4 = project_three(normed4, qkv4)
    paired4 = partner(projected4[1:], "grp", 0)
    key_rows4 = jnp.concatenate([projected4[1], paired4[0]], axis=0)
    value_rows4 = jnp.concatenate([projected4[2], paired4[1]], axis=0)
    attended4 = patch_attention(projected4[0], key_rows4, value_rows4, C4 // H4)
    fine_out = (
        curve_rows.astype(jnp.float32)
        + jnp.dot(attended4, proj4, preferred_element_type=jnp.float32)
    ).astype(jnp.bfloat16)
    block_start = pts_index * grp_count * fine_count
    valid_slot = mask5 > 0
    lifted = jnp.dot(
        lax.all_gather(fine_out, "grp", axis=0, tiled=True),
        pool_weight,
        preferred_element_type=jnp.float32,
    )
    picked = lifted[child5 - block_start]
    pooled_max = jnp.max(jnp.where(valid_slot[..., None], picked, -jnp.inf), axis=1)
    pooled = jax.nn.gelu(pooled_max, approximate=True).astype(jnp.bfloat16)
    coarse_count = child5.shape[0]
    coarse_width = pool_weight.shape[1]
    column_width = coarse_width // grp_count
    coarse_peer = coarse_count // pts_count
    coarse_owner = order5 // coarse_count
    coarse_sorted = jnp.argsort(coarse_owner, stable=True)
    coarse_wanted = (order5[coarse_sorted] - coarse_owner[coarse_sorted] * coarse_count).reshape(
        pts_count, coarse_peer
    )
    fetched = lax.all_to_all(
        pooled[lax.all_to_all(coarse_wanted, "pts", split_axis=0, concat_axis=0, tiled=True)],
        "pts",
        split_axis=0,
        concat_axis=0,
        tiled=True,
    )
    gathered_rows = fetched.reshape(coarse_count, pooled.shape[1])[jnp.argsort(coarse_sorted)]
    own_columns = lax.dynamic_slice_in_dim(gathered_rows, grp_index * column_width, column_width, 1)
    normed5 = layer_norm(gathered_rows, gain5)
    projected5 = project_three(normed5, qkv5)
    paired5 = partner(projected5[1:], "pts", 0)
    key_rows5 = jnp.concatenate([projected5[1], paired5[0]], axis=0)
    value_rows5 = jnp.concatenate([projected5[2], paired5[1]], axis=0)
    attended5 = patch_attention(projected5[0], key_rows5, value_rows5, C5 // H5)
    partial_terms = jnp.dot(attended5, proj5, preferred_element_type=jnp.float32)
    summed = lax.psum_scatter(
        partial_terms.astype(jnp.bfloat16), "grp", scatter_dimension=1, tiled=True
    ).astype(jnp.float32)
    coarse_out = (own_columns.astype(jnp.float32) + summed).astype(jnp.bfloat16)
    return (fine_out, coarse_out)


def solution(mesh):
    in_specs = (
        P(("pts", "grp"), None),
        P(("pts", "grp")),
        P(),
        P(),
        P(),
        P(),
        P("pts", None),
        P("pts", None),
        P("pts"),
        P(),
        P(None, None, "grp"),
        P("grp", None),
    )
    out_specs = (P(("pts", "grp"), None), P("pts", "grp"))
    return jax.shard_map(local, mesh=mesh, in_specs=in_specs, out_specs=out_specs, check_vma=False)
```

profile of v0, /device:TPU:1, one launch (start us, length us, event | category | flops | bytes accessed | tf_op | source)
XLA Modules:
  0.0 305.3 jit_solution(18006589911347884523)
XLA Ops:
  7.9 3.8 %sort.62 = (s32[512]{0:T(512)}, s32[512]{0:T(512)S(1)}) sort(s32[512]{0:T(512)S(1)} %add_select_fusion.1, s32[512]{0:T(512)S(1)} %iota.14), dimensions={0}, to_apply=%region_0.1 | sort | flops 4608 | bytes 8192 | tf_op jit(solution)/shard_map/jit(argsort)/sort | solution.py:79
  11.7 3.5 %gather_fusion.1 = s32[512]{0:T(512)S(1)} fusion(s32[512]{0:T(512)S(1)} %add_select_fusion.1, s32[1024]{0:T(1024)S(1)} %pad_clamp_fusion.5), kind=kCustom, calls=%fused_computation.1 | custom fusion | bytes 6144 | tf_op jit(solution)/shard_map/gather | solution.py:80
  15.2 3.5 %gather_fusion = s32[512]{0:T(512)S(1)} fusion(s32[512]{0:T(512)S(1)} %copy-done.1, s32[1024]{0:T(1024)S(1)} %pad_clamp_fusion.5), kind=kCustom, calls=%fused_computation | custom fusion | bytes 6144 | tf_op jit(solution)/shard_map/gather | solution.py:80
  18.9 35.3 %all_to_all.34 = s32[128,4,1]{1,2,0:T(1,128)S(1)} all-to-all(s32[128,4,1]{1,2,0:T(1,128)S(1)} %bitcast.131), channel_id=1, replica_groups=mesh['pts'=128,'grp'=4] {'pts'}, dimensions={0} | all-to-all | bytes 4096 | tf_op jit(solution)/shard_map/all_to_all | solution.py:84
  54.2 7.9 %all_to_all.35 = s32[128,4,1]{0,2,1:T(1,128)S(1)} all-to-all(s32[128,4,1]{0,2,1:T(1,128)S(1)} %copy.26), channel_id=1, replica_groups=mesh['pts'=128,'grp'=4] {'grp'}, dimensions={1} | all-to-all | bytes 4096 | tf_op jit(solution)/shard_map/all_to_all | solution.py:83
  62.4 2.0 gather_fusion.2
  65.1 7.1 %all-to-all-start.2 = ((bf16[128,4,1,256]{3,1,2,0:T(4,128)(2,1)}), bf16[128,4,1,256]{3,1,2,0:T(4,128)(2,1)S(1)}, u32[]{:S(2)}, u32[]{:S(2)}) async-start(bf16[128,4,1,256]{3,1,2,0:T(4,128)(2,1)} %bitcast.12), calls=%async_computation.2 | async-start | bytes 524288 | tf_op jit(solution)/shard_map/all_to_all | solution.py:92
  72.2 3.8 %sort.63 = (s32[512]{0:T(512)}, s32[512]{0:T(512)S(1)}) sort(s32[512]{0:T(512)S(1)} %get-tuple-element.60, s32[512]{0:T(512)S(1)} %iota.15), dimensions={0}, to_apply=%region_1.2 | sort | flops 4608 | bytes 8192 | tf_op jit(solution)/shard_map/jit(argsort)/sort | solution.py:99
  76.0 16.8 %all-to-all-done.2 = bf16[128,4,1,256]{3,1,2,0:T(4,128)(2,1)S(1)} async-done(((bf16[128,4,1,256]{3,1,2,0:T(4,128)(2,1)}), bf16[128,4,1,256]{3,1,2,0:T(4,128)(2,1)S(1)}, u32[]{:S(2)}, u32[]{:S(2)}) %all-to-all-start.2) | async-done | bytes 262176 | tf_op jit(solution)/shard_map/all_to_all | solution.py:92
  93.6 3.4 %all-to-all-start.3 = ((bf16[128,4,1,256]{3,0,2,1:T(8,128)(2,1)}), bf16[128,4,1,256]{3,0,2,1:T(8,128)(2,1)S(1)}, u32[]{:S(2)}, u32[]{:S(2)}) async-start(bf16[128,4,1,256]{3,0,2,1:T(8,128)(2,1)} %copy.32), calls=%async_computation.3 | async-start | bytes 524288 | tf_op jit(solution)/shard_map/all_to_all | solution.py:91
  97.1 6.0 %all-to-all-done.3 = bf16[128,4,1,256]{3,0,2,1:T(8,128)(2,1)S(1)} async-done(((bf16[128,4,1,256]{3,0,2,1:T(8,128)(2,1)}), bf16[128,4,1,256]{3,0,2,1:T(8,128)(2,1)S(1)}, u32[]{:S(2)}, u32[]{:S(2)}) %all-to-all-start.3) | async-done | bytes 262176 | tf_op jit(solution)/shard_map/all_to_all | solution.py:91
  103.3 2.0 gather_fusion.3
  106.3 2.2 collective-permute-start
  108.6 11.5 %collective-permute-done = bf16[2,512,256]{1,2,0:T(8,128)(2,1)S(1)} collective-permute-done((bf16[2,512,256]{1,2,0:T(8,128)(2,1)S(1)}, bf16[2,512,256]{1,2,0:T(8,128)(2,1)S(1)}, u32[]{:S(2)}, u32[]{:S(2)}) %collective-permute-start) | collective-permute-done | bytes 524320 | tf_op jit(solution)/shard_map/ppermute | solution.py:24
  120.2 27.2 %while.20 = (s32[]{:T(128)}, bf16[16,512,16]{1,2,0:T(8,128)(2,1)S(1)}, bf16[16,512,16]{1,2,0:T(8,128)(2,1)S(1)}, bf16[16,1024,16]{1,2,0:T(8,128)(2,1)S(1)}, bf16[16,1024,16]{1,2,0:T(8,128)(2,1)S(1)}, /*index=5*/s32[]{:T(128)}) while((s32[]{:T(128)}, bf16[16,512,16]{1,2,0:T(8,128)(2,1)S(1)}, bf16[16,512,16]{1,2,0:T(8,128)(2,1)S(1)}, ...), condition=%wide.region_7.8_spmd, body=%wide.region_4.7_spmd.sunk | while | flops 38280192 | bytes 6402117 | solution.py:58
  148.5 3.8 %sort.64 = (s32[512]{0:T(512)}, s32[512]{0:T(512)S(1)}) sort(s32[512]{0:T(512)S(1)} %add_select_fusion, s32[512]{0:T(512)S(1)} %iota.16), dimensions={0}, to_apply=%region_9.10 | sort | flops 4608 | bytes 8192 | tf_op jit(solution)/shard_map/jit(argsort)/sort | solution.py:125
  152.3 3.5 %gather_fusion.6 = s32[512]{0:T(512)S(1)} fusion(s32[512]{0:T(512)S(1)} %add_select_fusion, s32[1024]{0:T(1024)S(1)} %pad_clamp_fusion.2), kind=kCustom, calls=%fused_computation.6 | custom fusion | bytes 6144 | tf_op jit(solution)/shard_map/gather | solution.py:126
  155.8 3.5 %gather_fusion.5 = s32[512]{0:T(512)S(1)} fusion(s32[512]{0:T(512)S(1)} %copy-done.2, s32[1024]{0:T(1024)S(1)} %pad_clamp_fusion.2), kind=kCustom, calls=%fused_computation.5 | custom fusion | bytes 6144 | tf_op jit(solution)/shard_map/gather | solution.py:126
  160.1 10.8 %all-to-all-start.4 = ((s32[128,1,4]{2,1,0:T(1,128)}), s32[128,1,4]{2,1,0:T(1,128)S(1)}, u32[]{:S(2)}, u32[]{:S(2)}) async-start(s32[128,1,4]{2,1,0:T(1,128)} %bitcast.26), calls=%async_computation.4 | async-start | bytes 131072 | tf_op jit(solution)/shard_map/all_to_all | solution.py:130
  171.4 14.3 %all-to-all-done.4 = s32[128,1,4]{2,1,0:T(1,128)S(1)} async-done(((s32[128,1,4]{2,1,0:T(1,128)}), s32[128,1,4]{2,1,0:T(1,128)S(1)}, u32[]{:S(2)}, u32[]{:S(2)}) %all-to-all-start.4) | async-done | bytes 2080 | tf_op jit(solution)/shard_map/all_to_all | solution.py:130
  186.0 3.9 %fusion.65 = f32[2048,512]{1,0:T(8,128)} fusion(bf16[2048,256]{1,0:T(8,128)(2,1)} %all-gather.2.cloned.1.call-done, bf16[256,512]{1,0:T(8,128)(2,1)S(1)} %copy-done.5), kind=kOutput, calls=%fused_computation.126 | convolution fusion | flops 536870912 | bytes 5505024 | tf_op jit(solution)/shard_map/dot_general | solution.py:112
  189.9 20.2 %gather_fusion.4 = f32[4096,512]{1,0:T(8,128)} fusion(f32[2048,512]{1,0:T(8,128)} %fusion.65, s32[4096]{0:T(1024)S(1)} %broadcast_clamp_fusion), kind=kCustom, calls=%fused_computation.4 | custom fusion | bytes 16793600 | tf_op jit(solution)/shard_map/gather | solution.py:117
  210.2 5.4 %fusion.26 = f32[512,512]{1,0:T(8,128)S(1)} fusion(f32[4096,512]{1,0:T(8,128)} %gather_fusion.4, pred[512,8]{1,0:T(8,128)(4,1)S(1)} %copy.35), kind=kLoop, calls=%fused_computation.44 | loop fusion | flops 3932160 | bytes 9441280 | tf_op jit(solution)/shard_map/reduce_max | solution.py:118
  215.9 2.0 gather_fusion.7
  218.8 5.7 %all-to-all-start.5 = ((bf16[128,4,512]{2,1,0:T(4,128)(2,1)}), bf16[128,4,512]{2,1,0:T(4,128)(2,1)S(1)}, u32[]{:S(2)}, u32[]{:S(2)}) async-start(bf16[128,4,512]{2,1,0:T(4,128)(2,1)} %reshape.208), calls=%async_computation.5 | async-start | bytes 1048576 | tf_op jit(solution)/shard_map/all_to_all | solution.py:129
  224.5 3.8 %sort.65 = (s32[512]{0:T(512)}, s32[512]{0:T(512)S(1)}) sort(s32[512]{0:T(512)S(1)} %get-tuple-element.63, s32[512]{0:T(512)S(1)} %iota.17), dimensions={0}, to_apply=%region_10.11 | sort | flops 4608 | bytes 8192 | tf_op jit(solution)/shard_map/jit(argsort)/sort | solution.py:136
  228.5 27.2 %all-to-all-done.5 = bf16[128,4,512]{2,1,0:T(4,128)(2,1)S(1)} async-done(((bf16[128,4,512]{2,1,0:T(4,128)(2,1)}), bf16[128,4,512]{2,1,0:T(4,128)(2,1)S(1)}, u32[]{:S(2)}, u32[]{:S(2)}) %all-to-all-start.5) | async-done | bytes 524320 | tf_op jit(solution)/shard_map/all_to_all | solution.py:129
  255.9 2.0 gather_fusion.8
  259.0 2.6 collective-permute-start.1
  261.7 1.1 collective-permute-done.1
  262.8 13.6 %while.21 = (s32[]{:T(128)}, bf16[8,512,16]{1,2,0:T(8,128)(2,1)S(1)}, bf16[8,512,16]{1,2,0:T(8,128)(2,1)S(1)}, bf16[8,1024,16]{1,2,0:T(8,128)(2,1)S(1)}, bf16[8,1024,16]{1,2,0:T(8,128)(2,1)S(1)}, /*index=5*/s32[]{:T(128)}) while((s32[]{:T(128)}, bf16[8,512,16]{1,2,0:T(8,128)(2,1)S(1)}, bf16[8,512,16]{1,2,0:T(8,128)(2,1)S(1)}, ...), condition=%wide.region_16.17_spmd, body=%wide.region_13.16_spmd.sunk | while | flops 38280192 | bytes 6402117 | solution.py:58
  277.8 18.9 %reduce-scatter.4.cloned.1.call-done = bf16[128,512]{1,0:T(8,128)(2,1)} async-done(((bf16[512,512]{1,0:T(8,128)(2,1)}), bf16[128,512]{1,0:T(8,128)(2,1)}) %reduce-scatter.4.cloned.1.call-update) | async-done | bytes 131088
  (170 shorter events, 53.4 us)
Async XLA Ops:
  7.2 98.5 %copy-start = (bf16[3,256,256]{2,1,0:T(8,128)(2,1)S(1)}, bf16[3,256,256]{2,1,0:T(8,128)(2,1)}, u32[]{:S(2)}) copy-start(bf16[3,256,256]{2,1,0:T(8,128)(2,1)} %param.19) | copy-start | bytes 1179652
  7.2 8.1 %copy-start.1 = (s32[512]{0:T(512)S(1)}, s32[512]{0:T(512)}, u32[]{:S(2)}) copy-start(s32[512]{0:T(512)} %param.17) | copy-start | bytes 6148
  11.7 50.6 %copy-start.3 = (bf16[512,256]{1,0:T(8,128)(2,1)S(1)}, bf16[512,256]{1,0:T(8,128)(2,1)}, u32[]{:S(2)}) copy-start(bf16[512,256]{1,0:T(8,128)(2,1)} %param.16) | copy-start | bytes 786436
  65.1 27.7 %all-to-all-start.2 = ((bf16[128,4,1,256]{3,1,2,0:T(4,128)(2,1)}), bf16[128,4,1,256]{3,1,2,0:T(4,128)(2,1)S(1)}, u32[]{:S(2)}, u32[]{:S(2)}) async-start(bf16[128,4,1,256]{3,1,2,0:T(4,128)(2,1)} %bitcast.12), calls=%async_computation.2 | async-start | bytes 524288 | tf_op jit(solution)/shard_map/all_to_all | solution.py:92
  93.6 9.5 %all-to-all-start.3 = ((bf16[128,4,1,256]{3,0,2,1:T(8,128)(2,1)}), bf16[128,4,1,256]{3,0,2,1:T(8,128)(2,1)S(1)}, u32[]{:S(2)}, u32[]{:S(2)}) async-start(bf16[128,4,1,256]{3,0,2,1:T(8,128)(2,1)} %copy.32), calls=%async_computation.3 | async-start | bytes 524288 | tf_op jit(solution)/shard_map/all_to_all | solution.py:91
  97.0 8.7 %copy-start.10 = (f32[256]{0:T(256)S(1)}, f32[256]{0:T(256)}, u32[]{:S(2)}) copy-start(f32[256]{0:T(256)} %param.18) | copy-start | bytes 3076
  97.0 89.0 %all-gather.2.cloned.1.call-start = ((), (), s32[]{:S(2)}) async-start(), calls=%async_computation.7 | async-start | bytes 1310720 | tf_op jit(solution)/shard_map/all_gather | solution.py:113
  106.3 13.8 %collective-permute-start = (bf16[2,512,256]{1,2,0:T(8,128)(2,1)S(1)}, bf16[2,512,256]{1,2,0:T(8,128)(2,1)S(1)}, u32[]{:S(2)}, u32[]{:S(2)}) collective-permute-start(bf16[2,512,256]{1,2,0:T(8,128)(2,1)S(1)} %slice.68), channel_id=1, source_target_pairs={{0,1},{1,0},{2,3},{3,2},{4,5},{5,4},{6,7},{7,6},{8,9},{9,8},{10,11... | collective-permute-start | bytes 1572872 | tf_op jit(solution)/shard_map/ppermute | solution.py:24
  120.2 27.2 %copy-start.6 = (bf16[256,256]{1,0:T(8,128)(2,1)S(1)}, bf16[256,256]{1,0:T(8,128)(2,1)}, u32[]{:S(2)}) copy-start(bf16[256,256]{1,0:T(8,128)(2,1)} %param.20) | copy-start | bytes 393220
  120.2 28.2 %copy-start.2 = (s32[512]{0:T(512)S(1)}, s32[512]{0:T(512)}, u32[]{:S(2)}) copy-start(s32[512]{0:T(512)} %param.24) | copy-start | bytes 6148
  152.3 18.6 %copy-start.9 = (s32[512,8]{0,1:T(8,128)S(1)}, s32[512,8]{0,1:T(8,128)}, u32[]{:S(2)}) copy-start(s32[512,8]{0,1:T(8,128)} %param.22) | copy-start | bytes 49156
  152.3 18.9 %copy-start.8 = (s32[512,8]{0,1:T(8,128)S(1)}, s32[512,8]{0,1:T(8,128)}, u32[]{:S(2)}) copy-start(s32[512,8]{0,1:T(8,128)} %param.23) | copy-start | bytes 49156
  155.8 30.2 %copy-start.5 = (bf16[256,512]{1,0:T(8,128)(2,1)S(1)}, bf16[256,512]{1,0:T(8,128)(2,1)}, u32[]{:S(2)}) copy-start(bf16[256,512]{1,0:T(8,128)(2,1)} %param.21) | copy-start | bytes 786436
  160.1 25.6 %all-to-all-start.4 = ((s32[128,1,4]{2,1,0:T(1,128)}), s32[128,1,4]{2,1,0:T(1,128)S(1)}, u32[]{:S(2)}, u32[]{:S(2)}) async-start(s32[128,1,4]{2,1,0:T(1,128)} %bitcast.26), calls=%async_computation.4 | async-start | bytes 131072 | tf_op jit(solution)/shard_map/all_to_all | solution.py:130
  217.9 10.4 %copy-start.4 = (bf16[3,512,128]{2,1,0:T(8,128)(2,1)S(1)}, bf16[3,512,128]{2,1,0:T(8,128)(2,1)}, u32[]{:S(2)}) copy-start(bf16[3,512,128]{2,1,0:T(8,128)(2,1)} %param.26) | copy-start | bytes 1179652
  218.8 37.0 %all-to-all-start.5 = ((bf16[128,4,512]{2,1,0:T(4,128)(2,1)}), bf16[128,4,512]{2,1,0:T(4,128)(2,1)S(1)}, u32[]{:S(2)}, u32[]{:S(2)}) async-start(bf16[128,4,512]{2,1,0:T(4,128)(2,1)} %reshape.208), calls=%async_computation.5 | async-start | bytes 1048576 | tf_op jit(solution)/shard_map/all_to_all | solution.py:129
  224.5 72.2 %reduce-scatter.4.cloned.1.call-start = ((), (), s32[]{:S(2)}) async-start(), calls=%async_computation.8 | async-start | bytes 655360
  255.9 2.5 copy-start.11
  259.0 3.8 %collective-permute-start.1 = (bf16[2,512,128]{1,2,0:T(8,128)(2,1)S(1)}, bf16[2,512,128]{1,2,0:T(8,128)(2,1)S(1)}, u32[]{:S(2)}, u32[]{:S(2)}) collective-permute-start(bf16[2,512,128]{1,2,0:T(8,128)(2,1)S(1)} %slice.74), channel_id=1, source_target_pairs={{0,4},{4,0},{8,12},{12,8},{16,20},{20,16},{24,28},{28,24},{32,36},... | collective-permute-start | bytes 786440 | tf_op jit(solution)/shard_map/ppermute | solution.py:24
  262.8 13.6 %copy-start.7 = (bf16[128,512]{1,0:T(8,128)(2,1)S(1)}, bf16[128,512]{1,0:T(8,128)(2,1)}, u32[]{:S(2)}) copy-start(bf16[128,512]{1,0:T(8,128)(2,1)} %param.27) | copy-start | bytes 393220
Sparse Core Ops, SparseCore 0:
  148.6 24.2 all-gather.1
  277.9 18.7 reduce-scatter.3
where the time goes:
time: 307 us; the launch traced here: 305 us
  waiting for transfers between devices  95.9 us (31%)
  local copies, waits for them, and re-layouts  49.2 us (16%)
  blocking collectives  43.2 us (14%)
  other arithmetic  36 us (12%)
  matrix products  34.5 us (11%)
  starting transfers between devices  31.8 us (10%)
  between operations  14.7 us (5%)
    all_to_all x1, blocking collectives, local(): lax.all_to_all(wanted, 'pts', split_axis=0, concat_axis=0, tiled=True)  35.3 us
    all_to_all x1, waiting for transfers between devices, local(): lax.all_to_all(pooled[lax.all_to_all(coarse_wanted, 'pts', split_axis=0,...  27.2 us
    gather x1, local copies, waits for them, and re-layouts, local(): picked = lifted[child5 - block_start]  20.2 us
    unnamed x3, waiting for transfers between devices  18.9 us
    all_to_all x1, waiting for transfers between devices, local(): lax.all_to_all(outgoing, 'pts', split_axis=0, concat_axis=0, tiled=True)  16.8 us
    dot_general x24, matrix products, one_head(): jnp.dot(probabilities, value_rows, preferred_element_type=jnp.float32)  15 us
    all_to_all x1, waiting for transfers between devices, local(): lax.all_to_all(coarse_wanted, 'pts', split_axis=0, concat_axis=0, tiled=T...  14.3 us
    dot_general x24, matrix products, one_head(): jnp.einsum('qd,kd->qk', queries, key_rows, preferred_element_type=jnp.flo...  13.2 us
  transfers between devices with their start and end apart: 8, of which 7 were waited for; matrix products, arithmetic and copies ran while one was open for 7% of the time, Pallas kernels for 0%

commit v1 on v0

v1 whole, which is shorter than its diff:
```python
import functools
import math

import jax
import jax.numpy as jnp
from jax import lax
from jax.experimental import pallas as pl
from jax.experimental.pallas import tpu as pltpu
from jax.sharding import Mesh
from jax.sharding import PartitionSpec as P

C4 = 256
H4 = 16
C5 = 512
H5 = 32
HEAD = 16
KIDS = 8

epsilon = 1e-05
f32 = jnp.float32
bf16 = jnp.bfloat16

PTS = ("z", "y", "c")
PLANE = ("y", "c", "x")
ALL = ("z", "y", "c", "x")


def dot(a, b):
    return jnp.dot(a, b, preferred_element_type=f32)


def column(row):
    return jnp.transpose(jnp.broadcast_to(row, (8, row.shape[1])))[:, :1]


def one_hot(col, width):
    lanes = lax.broadcasted_iota(jnp.int32, (col.shape[0], width), 1)
    return jnp.where(col == lanes, 1.0, 0.0).astype(bf16)


def layer_norm(rows_in, norm_gain):
    values = rows_in.astype(f32)
    center = values - jnp.mean(values, axis=-1, keepdims=True)
    spread = jnp.mean(center * center, axis=-1, keepdims=True)
    return (center * lax.rsqrt(spread + epsilon) * norm_gain).astype(bf16)


def params(mib=48):
    return pltpu.CompilerParams(vmem_limit_bytes=mib << 20)


def request_kernel(order4_ref, order5_ref, out_ref, slot_ref):
    n = order4_ref.shape[1]
    x = lax.axis_index("x")
    owner4 = column(order4_ref[...] // n)
    rem4 = column(order4_ref[...] % n).astype(f32)
    lanes = lax.broadcasted_iota(jnp.int32, (n, n), 1)
    rows = lax.broadcasted_iota(jnp.int32, (n, n), 0)
    want4 = jnp.sum(jnp.where(owner4 == lanes, rem4, 0.0), axis=0, keepdims=True)
    owner5_row = order5_ref[...] // n
    owner5 = column(owner5_row)
    rem5 = column(order5_ref[...] % n).astype(f32)
    earlier = jnp.where((owner5 == owner5_row) & (rows < lanes), 1.0, 0.0)
    rank_row = jnp.sum(earlier, axis=0, keepdims=True).astype(jnp.int32)
    rank = column(rank_row)
    mine = (owner5 == lanes // 4) & (rank == x)
    want5 = jnp.sum(jnp.where(mine, rem5, 0.0), axis=0, keepdims=True)
    out_ref[...] = jnp.concatenate([want4, want5], axis=0).astype(jnp.int32)
    slot_ref[...] = owner5_row * 4 + rank_row


def pick_kernel(index_ref, table_ref, out_ref):
    out_ref[...] = dot(one_hot(column(index_ref[...]), table_ref.shape[0]), table_ref[...]).astype(
        bf16
    )


def norm4_kernel(order4_ref, arrived_ref, gain_ref, rows_ref, normed_ref):
    n = arrived_ref.shape[0]
    rows = dot(one_hot(column(order4_ref[...] // n), n), arrived_ref[...]).astype(bf16)
    rows_ref[...] = rows
    normed_ref[...] = layer_norm(rows, gain_ref[...])


def attend(heads, k_ref, qt_ref, vt_ref, at_ref, s_ref, chunk=512):
    width = heads * HEAD
    queries = qt_ref.shape[1]
    keys = k_ref.shape[0]
    row_head = lax.broadcasted_iota(jnp.int32, (width, queries), 0) // HEAD

    def of_head(head):
        q = qt_ref[...]
        return jnp.where(row_head == head, q, jnp.zeros_like(q))

    def score(q_head, slot, c, top):
        s = dot(k_ref[c * chunk : (c + 1) * chunk, :], q_head)
        s_ref[slot, c * chunk : (c + 1) * chunk, :] = s
        return jnp.maximum(top, jnp.max(s.reshape(chunk // 8, 8, queries), axis=0))

    def low():
        return jnp.full((8, queries), -jnp.inf, f32)

    def step(head, slot, peak, more):
        mixed = jnp.zeros((2 * HEAD, queries), f32)
        top = low()
        q_next = of_head(head + 1) if more else None
        for c in range(keys // chunk):
            if more:
                top = score(q_next, 1 - slot, c, top)
            p = jnp.exp(s_ref[slot, c * chunk : (c + 1) * chunk, :] - peak).astype(bf16)
            mixed = mixed + dot(vt_ref[head, :, c * chunk : (c + 1) * chunk], p)
        at_ref[head] = (mixed[:HEAD] / mixed[HEAD:]).astype(bf16)
        return jnp.max(top, axis=0, keepdims=True)

    top = low()
    q_first = of_head(0)
    for c in range(keys // chunk):
        top = score(q_first, 0, c, top)
    peak = jnp.max(top, axis=0, keepdims=True)

    def pair(i, peak):
        peak = step(2 * i, 0, peak, True)
        return step(2 * i + 1, 1, peak, True)

    peak = lax.fori_loop(0, heads // 2 - 1, pair, peak)
    peak = step(heads - 2, 0, peak, True)
    step(heads - 1, 1, peak, False)
    return jnp.transpose(at_ref[...].reshape(width, queries))


def attend_scratch(heads, queries, keys):
    width = heads * HEAD
    return [
        pltpu.VMEM((keys, width), bf16),
        pltpu.VMEM((width, queries), bf16),
        pltpu.VMEM((heads, 2 * HEAD, keys), bf16),
        pltpu.VMEM((heads, HEAD, queries), bf16),
        pltpu.VMEM((2, keys, queries), f32),
    ]


def load_values(vt_ref, values, heads):
    keys = values.shape[0]
    vt_ref[:, :HEAD, :] = jnp.transpose(values).reshape(heads, HEAD, keys)
    vt_ref[:, HEAD:, :] = jnp.ones((heads, HEAD, keys), bf16)


SCALE = 1.0 / math.sqrt(HEAD)


def fine_kernel(own_ref, other_ref, rows_ref, qkv_ref, proj_ref, out_ref, k, qt, vt, at, s):
    n = own_ref.shape[0]
    own, other = own_ref[...], other_ref[...]
    query = dot(own, qkv_ref[0]).astype(bf16) * bf16(SCALE)
    qt[...] = jnp.transpose(query)
    k[:n] = dot(own, qkv_ref[1]).astype(bf16)
    k[n:] = dot(other, qkv_ref[1]).astype(bf16)
    values = jnp.concatenate([dot(own, qkv_ref[2]), dot(other, qkv_ref[2])], axis=0)
    load_values(vt, values.astype(bf16), H4)
    attended = attend(H4, k, qt, vt, at, s)
    out_ref[...] = (rows_ref[...].astype(f32) + dot(attended, proj_ref[...])).astype(bf16)


def coarse_kernel(q_ref, own_ref, other_ref, proj_ref, out_ref, k, qt, vt, at, s):
    n, width = q_ref.shape
    qt[...] = jnp.transpose(q_ref[...] * bf16(SCALE))
    k[:n] = own_ref[:, :width]
    k[n:] = other_ref[:, :width]
    values = jnp.concatenate([own_ref[:, width:], other_ref[:, width:]], axis=0)
    load_values(vt, values, width // HEAD)
    attended = attend(width // HEAD, k, qt, vt, at, s)
    terms = dot(attended, proj_ref[...]).astype(bf16)
    parts = out_ref.shape[0]
    for g in range(parts):
        out_ref[g] = terms[:, g * width : (g + 1) * width]


def pool_kernel(fine_ref, weight_ref, child_ref, index_ref, base_ref, out_ref):
    total = fine_ref.shape[0]
    points = child_ref.shape[1]
    width = weight_ref.shape[1]
    lifted = dot(fine_ref[...], weight_ref[...])
    start_row = child_ref[0:1, :] - base_ref[0]
    start = column(start_row)
    rows = lax.broadcasted_iota(jnp.int32, (total, points), 0)
    first = jnp.where(start_row == rows, 1.0, 0.0).astype(bf16)
    opens = dot(first, jnp.ones((points, width), bf16))

    def ahead(block, k):
        return jnp.concatenate([block[k:], jnp.ones((k, width), f32)], axis=0)

    cut = ahead(opens, 1)
    best = lifted
    reach = 1
    while reach < KIDS:
        best = jnp.where(cut > 0.0, best, jnp.maximum(best, ahead(best, reach)))
        cut = jnp.maximum(cut, ahead(cut, reach))
        reach *= 2
    pooled_rows = jax.nn.gelu(best, approximate=True).astype(bf16)
    pooled = dot(one_hot(start, total), pooled_rows).astype(bf16)
    out_ref[...] = dot(one_hot(column(index_ref[...]), points), pooled).astype(bf16)


def norm5_kernel(slot_ref, parts_ref, own_ref, gain_ref, qkv_ref, q_ref, kv_ref, cols_ref):
    n = slot_ref.shape[1]
    width = own_ref.shape[1]
    pick = one_hot(column(slot_ref[...]), n)
    rows = jnp.concatenate(
        [dot(pick, parts_ref[g]).astype(bf16) for g in range(parts_ref.shape[0])], axis=1
    )
    cols_ref[...] = dot(pick, own_ref[...]).astype(bf16)
    normed = layer_norm(rows, gain_ref[...])
    q_ref[...] = dot(normed, qkv_ref[0]).astype(bf16)
    kv_ref[:, :width] = dot(normed, qkv_ref[1]).astype(bf16)
    kv_ref[:, width:] = dot(normed, qkv_ref[2]).astype(bf16)


def sum_kernel(cols_ref, parts_ref, out_ref):
    total = cols_ref[...].astype(f32)
    summed = parts_ref[0].astype(f32)
    for g in range(1, parts_ref.shape[0]):
        summed = summed + parts_ref[g].astype(f32)
    out_ref[...] = (total + summed).astype(bf16)


def shape(dims, dtype=bf16):
    return jax.ShapeDtypeStruct(dims, dtype)


def exchange(block, axes):
    return lax.all_to_all(block, axes, split_axis=0, concat_axis=0, tiled=True)


def local(
    feats4, order4, gain4, qkv4, proj4, pool_weight, child5, mask5, order5, gain5, qkv5, proj5
):
    n = feats4.shape[0]
    nz = lax.axis_size("z")
    plane = lax.axis_size("y") * lax.axis_size("c") * lax.axis_size("x")
    nx = lax.axis_size("x")
    pts_count = nz * lax.axis_size("y") * lax.axis_size("c")
    pts_index = lax.axis_index(PTS)
    grp_index = lax.axis_index("x")
    order4_row = order4.reshape(1, n)

    wanted, slots = pl.pallas_call(
        request_kernel,
        out_shape=[shape((2, n), jnp.int32), shape((1, n), jnp.int32)],
        compiler_params=params(),
        name="request",
    )(order4_row, order5.reshape(1, n))
    by_z = exchange(wanted.reshape(2, nz, plane).transpose(1, 0, 2), ("z",))
    by_plane = exchange(by_z.transpose(2, 1, 0), PLANE)
    asked = by_plane.transpose(1, 2, 0).reshape(2, n)

    outgoing = pl.pallas_call(
        pick_kernel, out_shape=shape((n, C4)), compiler_params=params(), name="pick4"
    )(asked[0:1], feats4)
    arrived = exchange(outgoing, ALL)
    curve_rows, normed4 = pl.pallas_call(
        norm4_kernel,
        out_shape=[shape((n, C4)), shape((n, C4))],
        compiler_params=params(),
        name="norm4",
    )(order4_row, arrived, gain4.reshape(1, C4))
    other4 = lax.ppermute(normed4, "x", [(i, i ^ 1) for i in range(nx)])
    fine_out = pl.pallas_call(
        fine_kernel,
        out_shape=shape((n, C4)),
        scratch_shapes=attend_scratch(H4, n, 2 * n),
        compiler_params=params(),
        name="attend4",
    )(normed4, other4, curve_rows, qkv4, proj4)

    width = C5 // nx
    fine_all = exchange(jnp.broadcast_to(fine_out[None], (nx, n, C4)), "x").reshape(nx * n, C4)
    base = (pts_index * (nx * n)).reshape(1).astype(jnp.int32)
    own_weight = lax.dynamic_slice_in_dim(pool_weight, grp_index * width, width, 1)
    smem = pl.BlockSpec(memory_space=pltpu.SMEM)
    vmem = pl.BlockSpec(memory_space=pltpu.VMEM)
    pooled = pl.pallas_call(
        pool_kernel,
        out_shape=shape((n, width)),
        in_specs=[vmem, vmem, vmem, vmem, smem],
        compiler_params=params(),
        name="pool",
    )(fine_all, own_weight, child5.T, asked[1:2], base)
    own_part = exchange(pooled.reshape(pts_count, n // pts_count, width), PTS).reshape(n, width)
    parts = exchange(jnp.broadcast_to(own_part[None], (nx, n, width)), "x")
    query5, kv5, own_columns = pl.pallas_call(
        norm5_kernel,
        out_shape=[shape((n, width)), shape((n, 2 * width)), shape((n, width))],
        compiler_params=params(),
        name="norm5",
    )(slots, parts, own_part, gain5.reshape(1, C5), qkv5)
    other5 = lax.ppermute(kv5, "c", [(0, 1), (1, 0)])
    terms = pl.pallas_call(
        coarse_kernel,
        out_shape=shape((nx, n, width)),
        scratch_shapes=attend_scratch(width // HEAD, n, 2 * n),
        compiler_params=params(),
        name="attend5",
    )(query5, kv5, other5, proj5)
    summed = exchange(terms, "x")
    coarse_out = pl.pallas_call(
        sum_kernel, out_shape=shape((n, width)), compiler_params=params(), name="add5"
    )(own_columns, summed)
    return (fine_out, coarse_out)


def solution(mesh):
    pts, grp = mesh.devices.shape
    inner = Mesh(mesh.devices.reshape(pts // 8, 4, 2, grp), ALL)
    in_specs = (
        P(ALL, None),
        P(ALL),
        P(),
        P(),
        P(),
        P(),
        P(PTS, None),
        P(PTS, None),
        P(PTS),
        P(),
        P(None, None, "x"),
        P("x", None),
    )
    out_specs = (P(ALL, None), P(PTS, "x"))
    return jax.shard_map(local, mesh=inner, in_specs=in_specs, out_specs=out_specs, check_vma=False)
```

time: 307 us -> 188 us (0.61)
  blocking collectives: 43.2 us -> 123 us
  waiting for transfers between devices: 95.9 us -> 23.1 us
  local copies, waits for them, and re-layouts: 49.2 us -> 6.14 us
  other arithmetic: 36 us -> 0.81 us
  matrix products: 34.5 us -> 0 us
  Pallas kernels: 0 us -> 24.1 us
  starting transfers between devices: 31.8 us -> 8.89 us
  between operations: 14.7 us -> 0.83 us
    all_to_all x2 -> x6, blocking collectives: 43.2 us -> 123 us  [exchange(): return lax.all_to_all(block, axes, split_axis=0, concat_axis=0, tiled=True)]
    all_to_all x4 -> x1, waiting for transfers between devices: 64.3 us -> 14.8 us  [exchange(): return lax.all_to_all(block, axes, split_axis=0, concat_axis=0, tiled=True)]
    gather x11 -> x0, local copies, waits for them, and re-layouts: 43.7 us -> none  [the longest x1 20.2 us: local(): picked = lifted[child5 - block_start]]
    dot_general x52 -> x0, matrix products: 33.9 us -> none  [the longest x24 15 us: one_head(): jnp.dot(probabilities, value_rows, preferred_element_type=jnp.float32)]
    pallas_call x0 -> x8, Pallas kernels: none -> 24.1 us  [the longest x1 11 us: local(): pl.pallas_call(fine_kernel, out_shape=shape((n, C4)), scratch_shapes=atte...]
    all_to_all x4 -> x1, starting transfers between devices: 27 us -> 3.51 us  [exchange(): return lax.all_to_all(block, axes, split_axis=0, concat_axis=0, tiled=True)]
    unnamed x3 -> x0, waiting for transfers between devices: 18.9 us -> none
    sort x4 -> x0, other arithmetic: 15.1 us -> none  [the longest x1 3.77 us: local(): sorted_slots = jnp.argsort(owner_flat, stable=True)]
  transfers between devices with their start and end apart: 8 -> 3, of which waited for: 7 -> 3; matrix products, arithmetic and copies ran while one was open for 7% -> 0% of each run, Pallas kernels for 0% -> 0%
where the time goes in v1:
time: 188 us; the launch traced here: 187 us
  blocking collectives  123 us (65%)
  Pallas kernels  24.1 us (13%)
  waiting for transfers between devices  23.1 us (12%)
  starting transfers between devices  8.89 us (5%)
  local copies, waits for them, and re-layouts  6.14 us (3%)
    all_to_all x6, blocking collectives, exchange(): return lax.all_to_all(block, axes, split_axis=0, concat_axis=0, tiled=True)  123 us
    all_to_all x1, waiting for transfers between devices, exchange(): return lax.all_to_all(block, axes, split_axis=0, concat_axis=0, tiled=True)  14.8 us
    pallas_call x1, Pallas kernels, local(): pl.pallas_call(fine_kernel, out_shape=shape((n, C4)), scratch_shapes=atte...  11 us
    ppermute x1, waiting for transfers between devices, local(): other4 = lax.ppermute(normed4, 'x', [(i, i ^ 1) for i in range(nx)])  7.1 us
    pallas_call x1, Pallas kernels, local(): pl.pallas_call(coarse_kernel, out_shape=shape((nx, n, width)), scratch_sh...  5.07 us
  transfers between devices with their start and end apart: 3, of which 3 were waited for; matrix products, arithmetic and copies ran while one was open for 0% of the time, Pallas kernels for 0%

profile of v1, /device:TPU:1, one launch (start us, length us, event | category | flops | bytes accessed | tf_op | source)
XLA Modules:
  0.0 187.2 jit_solution(5181179170678387824)
XLA Ops:
  0.7 0.7 copy-done.7
  1.4 0.7 copy-done.9
  2.1 1.1 request.1
  3.1 0.1 reshape.38
  3.2 26.9 %all_to_all.41 = s32[16,2,32]{2,1,0:T(2,128)S(1)} all-to-all(s32[16,2,32]{2,1,0:T(2,128)S(1)} %bitcast.32), channel_id=1, replica_groups=mesh['z'=16,'y'=4,'c'=2,'x'=4] {'z'}, dimensions={0} | all-to-all | bytes 8192 | tf_op jit(solution)/shard_map/all_to_all | solution.py:231
  30.2 0.1 copy.19
  30.3 16.2 %all_to_all.42 = s32[32,2,16]{2,1,0:T(2,128)S(1)} all-to-all(s32[32,2,16]{2,1,0:T(2,128)S(1)} %copy.19), channel_id=1, replica_groups=mesh['z'=16,'y'=4,'c'=2,'x'=4] {'y','c','x'}, dimensions={0} | all-to-all | bytes 8192 | tf_op jit(solution)/shard_map/all_to_all | solution.py:231
  46.5 0.1 slice.13.index_ref
  46.6 0.6 pick4.1
  47.2 0.5 broadcast.1
  47.7 0.8 reduce
  48.6 34.1 %all_to_all.43 = bf16[512,2,128]{2,1,0:T(2,128)(2,1)S(1)} all-to-all(bf16[512,2,128]{2,1,0:T(2,128)(2,1)S(1)} %reshape.44), channel_id=1, replica_groups=mesh['z'=16,'y'=4,'c'=2,'x'=4] {'z','y','c','x'}, dimensions={0} | all-to-all | bytes 524288 | tf_op jit(solution)/shard_map/all_to_all | solution.py:231
  82.6 0.1 reshape.45
  82.9 0.7 copy-done.10
  83.6 0.7 norm4.1
  84.3 2.2 %collective-permute-start = (bf16[512,256]{1,0:T(8,128)(2,1)S(1)}, bf16[512,256]{1,0:T(8,128)(2,1)S(1)}, u32[]{:S(2)}, u32[]{:S(2)}) collective-permute-start(bf16[512,256]{1,0:T(8,128)(2,1)S(1)} %get-tuple-element.10.own_ref), channel_id=1, source_target_pairs={{0,1},{1,0},{2,3},{3,2},{4,5},{5,4},{6,7},{7,6},{8,9},{9,8},{10,11... | collective-permute-start | bytes 786440 | tf_op jit(solution)/shard_map/ppermute | solution.py:266
  86.6 7.1 %collective-permute-done.other_ref = bf16[512,256]{1,0:T(8,128)(2,1)S(1)} collective-permute-done((bf16[512,256]{1,0:T(8,128)(2,1)S(1)}, bf16[512,256]{1,0:T(8,128)(2,1)S(1)}, u32[]{:S(2)}, u32[]{:S(2)}) %collective-permute-start) | collective-permute-done | bytes 262176 | tf_op jit(solution)/shard_map/ppermute | solution.py:266
  93.7 11.0 %attend4.1 = bf16[512,256]{1,0:T(8,128)(2,1)} custom-call(bf16[512,256]{1,0:T(8,128)(2,1)S(1)} %get-tuple-element.10.own_ref, bf16[512,256]{1,0:T(8,128)(2,1)S(1)} %collective-permute-done.other_ref, bf16[512,256]{1,0:T(8,128)(2,1)S(1)} %get-tuple-element.11.rows_ref, bf16[3,256,256]{2,1,0:T(8,128)(2,1)S(1)} %copy-done.1, bf16[256,256]{1,0:T(8,128)(2,1)S(1)} %copy-done.4), custom_call_target="tpu_custom_call" | custom-call | tf_op jit(solution)/shard_map/attend4/pallas_call | solution.py:267
  104.6 2.0 %broadcast_in_dim.6 = bf16[4,512,256]{2,1,0:T(8,128)(2,1)} broadcast(bf16[512,256]{1,0:T(8,128)(2,1)} %attend4.1), dimensions={1,2} | broadcast | bytes 1310720 | tf_op jit(solution)/shard_map/broadcast_in_dim | solution.py:276
  106.6 3.5 %all-to-all-start.3 = ((bf16[4,512,256]{2,1,0:T(8,128)(2,1)}), bf16[4,512,256]{2,1,0:T(8,128)(2,1)S(1)}, u32[]{:S(2)}, u32[]{:S(2)}) async-start(bf16[4,512,256]{2,1,0:T(8,128)(2,1)} %broadcast_in_dim.6), calls=%async_computation.3 | async-start | bytes 2097152 | tf_op jit(solution)/shard_map/all_to_all | solution.py:231
  110.3 0.1 slice.15.index_ref
  110.4 14.8 %all-to-all-done.3 = bf16[4,512,256]{2,1,0:T(8,128)(2,1)S(1)} async-done(((bf16[4,512,256]{2,1,0:T(8,128)(2,1)}), bf16[4,512,256]{2,1,0:T(8,128)(2,1)S(1)}, u32[]{:S(2)}, u32[]{:S(2)}) %all-to-all-start.3) | async-done | bytes 1048608 | tf_op jit(solution)/shard_map/all_to_all | solution.py:231
  125.2 3.1 %pool.1 = bf16[512,128]{1,0:T(8,128)(2,1)S(1)} custom-call(bf16[2048,256]{1,0:T(8,128)(2,1)S(1)} %bitcast.18, bf16[256,128]{1,0:T(8,128)(2,1)S(1)} %constant_dynamic-slice_fusion.weight_ref, s32[8,512]{1,0:T(8,128)S(1)} %bitcast.24, s32[1,512]{1,0:T(1,128)S(1)} %slice.15.index_ref, s32[1]{0:T(128)} %bitcast.9.base_ref), custom_call_target="tpu_custom_call" | custom-call | tf_op jit(solution)/shard_map/pool/pallas_call | solution.py:281
  128.3 22.8 %all_to_all.44 = bf16[128,4,128]{2,1,0:T(4,128)(2,1)S(1)} all-to-all(bf16[128,4,128]{2,1,0:T(4,128)(2,1)S(1)} %bitcast.23), channel_id=1, replica_groups=mesh['z'=16,'y'=4,'c'=2,'x'=4] {'z','y','c'}, dimensions={0} | all-to-all | bytes 262144 | tf_op jit(solution)/shard_map/all_to_all | solution.py:231
  151.2 11.7 %all_to_all.45.parts_ref = bf16[4,512,128]{2,1,0:T(8,128)(2,1)S(1)} all-to-all(bf16[4,512,128]{2,1,0:T(8,128)(2,1)S(1)} %broadcast_in_dim.15), channel_id=1, replica_groups=mesh['z'=16,'y'=4,'c'=2,'x'=4] {'x'}, dimensions={0} | all-to-all | bytes 1048576 | tf_op jit(solution)/shard_map/all_to_all | solution.py:231
  162.9 0.7 copy-done.8
  163.6 1.8 norm5.1
  165.4 3.1 %collective-permute-start.1 = (bf16[512,256]{1,0:T(8,128)(2,1)S(1)}, bf16[512,256]{1,0:T(8,128)(2,1)S(1)}, u32[]{:S(2)}, u32[]{:S(2)}) collective-permute-start(bf16[512,256]{1,0:T(8,128)(2,1)S(1)} %get-tuple-element.15.own_ref), channel_id=1, source_target_pairs={{0,4},{4,0},{1,5},{5,1},{2,6},{6,2},{3,7},{7,3},{8,12},{12,8},{9,1... | collective-permute-start | bytes 786440 | tf_op jit(solution)/shard_map/ppermute | solution.py:296
  168.6 1.1 collective-permute-done.1.other_ref
  169.7 5.1 %attend5.1 = bf16[4,512,128]{2,1,0:T(8,128)(2,1)S(1)} custom-call(bf16[512,128]{1,0:T(8,128)(2,1)S(1)} %get-tuple-element.14.q_ref, bf16[512,256]{1,0:T(8,128)(2,1)S(1)} %get-tuple-element.15.own_ref, bf16[512,256]{1,0:T(8,128)(2,1)S(1)} %collective-permute-done.1.other_ref, bf16[128,512]{1,0:T(8,128)(2,1)S(1)} %copy-done.5), custom_call_target="tpu_custom_call" | custom-call | tf_op jit(solution)/shard_map/attend5/pallas_call | solution.py:297
  174.8 11.6 %all_to_all.46.parts_ref = bf16[4,512,128]{2,1,0:T(8,128)(2,1)S(1)} all-to-all(bf16[4,512,128]{2,1,0:T(8,128)(2,1)S(1)} %attend5.1), channel_id=1, replica_groups=mesh['z'=16,'y'=4,'c'=2,'x'=4] {'x'}, dimensions={0} | all-to-all | bytes 1048576 | tf_op jit(solution)/shard_map/all_to_all | solution.py:231
  186.4 0.7 add5.1
  (26 shorter events, 0.4 us)
Async XLA Ops:
  0.6 109.5 %copy-start = (bf16[256,512]{1,0:T(8,128)(2,1)S(1)}, bf16[256,512]{1,0:T(8,128)(2,1)}, u32[]{:S(2)}) copy-start(bf16[256,512]{1,0:T(8,128)(2,1)} %param.17) | copy-start | bytes 786436
  0.6 0.7 copy-start.7
  0.7 45.9 %copy-start.3 = (bf16[512,256]{1,0:T(8,128)(2,1)S(1)}, bf16[512,256]{1,0:T(8,128)(2,1)}, u32[]{:S(2)}) copy-start(bf16[512,256]{1,0:T(8,128)(2,1)} %table_ref.1) | copy-start | bytes 786436
  1.4 0.7 copy-start.9
  82.8 10.9 %copy-start.1 = (bf16[3,256,256]{2,1,0:T(8,128)(2,1)S(1)}, bf16[3,256,256]{2,1,0:T(8,128)(2,1)}, u32[]{:S(2)}) copy-start(bf16[3,256,256]{2,1,0:T(8,128)(2,1)} %qkv_ref.2) | copy-start | bytes 1179652
  82.8 0.7 copy-start.10
  83.6 10.1 %copy-start.4 = (bf16[256,256]{1,0:T(8,128)(2,1)S(1)}, bf16[256,256]{1,0:T(8,128)(2,1)}, u32[]{:S(2)}) copy-start(bf16[256,256]{1,0:T(8,128)(2,1)} %proj_ref.2) | copy-start | bytes 393220
  84.3 9.3 %collective-permute-start = (bf16[512,256]{1,0:T(8,128)(2,1)S(1)}, bf16[512,256]{1,0:T(8,128)(2,1)S(1)}, u32[]{:S(2)}, u32[]{:S(2)}) collective-permute-start(bf16[512,256]{1,0:T(8,128)(2,1)S(1)} %get-tuple-element.10.own_ref), channel_id=1, source_target_pairs={{0,1},{1,0},{2,3},{3,2},{4,5},{5,4},{6,7},{7,6},{8,9},{9,8},{10,11... | collective-permute-start | bytes 786440 | tf_op jit(solution)/shard_map/ppermute | solution.py:266
  106.6 18.6 %all-to-all-start.3 = ((bf16[4,512,256]{2,1,0:T(8,128)(2,1)}), bf16[4,512,256]{2,1,0:T(8,128)(2,1)S(1)}, u32[]{:S(2)}, u32[]{:S(2)}) async-start(bf16[4,512,256]{2,1,0:T(8,128)(2,1)} %broadcast_in_dim.6), calls=%async_computation.3 | async-start | bytes 2097152 | tf_op jit(solution)/shard_map/all_to_all | solution.py:231
  110.2 15.0 %copy-start.6 = (s32[512,8]{0,1:T(8,128)S(1)}, s32[512,8]{0,1:T(8,128)}, u32[]{:S(2)}) copy-start(s32[512,8]{0,1:T(8,128)} %param.18) | copy-start | bytes 49156
  151.2 11.8 %copy-start.2 = (bf16[3,512,128]{2,1,0:T(8,128)(2,1)S(1)}, bf16[3,512,128]{2,1,0:T(8,128)(2,1)}, u32[]{:S(2)}) copy-start(bf16[3,512,128]{2,1,0:T(8,128)(2,1)} %qkv_ref.3) | copy-start | bytes 1179652
  162.9 0.7 copy-start.8
  163.6 6.1 %copy-start.5 = (bf16[128,512]{1,0:T(8,128)(2,1)S(1)}, bf16[128,512]{1,0:T(8,128)(2,1)}, u32[]{:S(2)}) copy-start(bf16[128,512]{1,0:T(8,128)(2,1)} %proj_ref.3) | copy-start | bytes 393220
  165.4 4.3 %collective-permute-start.1 = (bf16[512,256]{1,0:T(8,128)(2,1)S(1)}, bf16[512,256]{1,0:T(8,128)(2,1)S(1)}, u32[]{:S(2)}, u32[]{:S(2)}) collective-permute-start(bf16[512,256]{1,0:T(8,128)(2,1)S(1)} %get-tuple-element.15.own_ref), channel_id=1, source_target_pairs={{0,4},{4,0},{1,5},{5,1},{2,6},{6,2},{3,7},{7,3},{8,12},{12,8},{9,1... | collective-permute-start | bytes 786440 | tf_op jit(solution)/shard_map/ppermute | solution.py:296

commit v2 on v1

v2 whole, which is shorter than its diff:
```python
import functools
import math

import jax
import jax.numpy as jnp
from jax import lax
from jax.experimental import pallas as pl
from jax.experimental.pallas import tpu as pltpu
from jax.sharding import Mesh
from jax.sharding import PartitionSpec as P

C4 = 256
H4 = 16
C5 = 512
H5 = 32
HEAD = 16
KIDS = 8

epsilon = 1e-05
f32 = jnp.float32
bf16 = jnp.bfloat16

PTS = ("z", "y", "c")
PLANE = ("y", "c", "x")
ALL = ("z", "y", "c", "x")


def dot(a, b):
    return jnp.dot(a, b, preferred_element_type=f32)


def column(row):
    return jnp.transpose(jnp.broadcast_to(row, (8, row.shape[1])))[:, :1]


def one_hot(col, width):
    lanes = lax.broadcasted_iota(jnp.int32, (col.shape[0], width), 1)
    return jnp.where(col == lanes, 1.0, 0.0).astype(bf16)


def layer_norm(rows_in, norm_gain):
    values = rows_in.astype(f32)
    center = values - jnp.mean(values, axis=-1, keepdims=True)
    spread = jnp.mean(center * center, axis=-1, keepdims=True)
    return (center * lax.rsqrt(spread + epsilon) * norm_gain).astype(bf16)


def fetch(pairs, sems):
    copies = [pltpu.make_async_copy(a, b, sems.at[i]) for i, (a, b) in enumerate(pairs)]
    for copy in copies:
        copy.start()
    return copies


def request_kernel(planes, order4_hbm, order5_hbm, out_ref, owner_ref, slot_ref, o4, o5, sems):
    for copy in fetch([(order4_hbm, o4), (order5_hbm, o5)], sems):
        copy.wait()
    n = o4.shape[1]
    nz, nx = out_ref.shape[0], lax.axis_size("x")
    x = lax.axis_index("x")
    owner4, owner5 = o4[...] // n, o5[...] // n
    owner_ref[...] = owner4
    owner5_col = column(owner5)
    lanes = lax.broadcasted_iota(jnp.int32, (n, n), 1)
    rows = lax.broadcasted_iota(jnp.int32, (n, n), 0)
    earlier = jnp.where((owner5_col == owner5) & (rows < lanes), 1.0, 0.0)
    rank = jnp.sum(earlier, axis=0, keepdims=True).astype(jnp.int32)
    per_z = planes // nx
    slot_ref[...] = ((owner5 % per_z) * nz + owner5 // per_z) * nx + rank

    lane = lax.broadcasted_iota(jnp.int32, (n, planes), 1)
    zs = lax.broadcasted_iota(jnp.int32, (nz, n), 0)

    def table(z_of, u_hit, row):
        z_hit = jnp.where(zs == z_of, 1.0, 0.0).astype(bf16)
        low = jnp.where(u_hit, (row % 256).astype(f32), 0.0).astype(bf16)
        high = jnp.where(u_hit, (row // 256).astype(f32), 0.0).astype(bf16)
        return dot(z_hit, low) + 256.0 * dot(z_hit, high)

    want4 = table(owner4 // planes, column(owner4 % planes) == lane, column(o4[...] % n))
    hit5 = (column(owner5 % per_z) == lane // nx) & (column(rank) == x)
    want5 = table(owner5 // per_z, hit5, column(o5[...] % n))
    out_ref[:, 0, :] = want4.astype(jnp.int32)
    out_ref[:, 1, :] = want5.astype(jnp.int32)


def pick_of(asked_ref, which, width):
    asked = asked_ref[:, which, :]
    cols = [asked[:, z : z + 1] for z in range(asked.shape[1])]
    return jnp.concatenate([one_hot(col, width) for col in cols], axis=0)


def pick_kernel(asked_ref, table_ref, out_ref):
    out_ref[...] = dot(pick_of(asked_ref, 0, table_ref.shape[0]), table_ref[...]).astype(bf16)


def norm4_kernel(owner_ref, arrived_ref, gain_hbm, rows_ref, normed_ref, gain, sems):
    copies = fetch([(gain_hbm, gain)], sems)
    n = arrived_ref.shape[0]
    rows = dot(one_hot(column(owner_ref[...]), n), arrived_ref[...]).astype(bf16)
    rows_ref[...] = rows
    copies[0].wait()
    normed_ref[...] = layer_norm(rows, gain[...])


def attend(heads, k_ref, qt_ref, vt_ref, s_ref, finish, before=None, chunk=512):
    width = heads * HEAD
    queries = qt_ref.shape[1]
    keys = k_ref.shape[0]
    row_head = lax.broadcasted_iota(jnp.int32, (width, queries), 0) // HEAD

    def of_head(head):
        q = qt_ref[...]
        return jnp.where(row_head == head, q, jnp.zeros_like(q))

    def score(q_head, slot, c, top):
        s = dot(k_ref[c * chunk : (c + 1) * chunk, :], q_head)
        s_ref[slot, c * chunk : (c + 1) * chunk, :] = s
        return jnp.maximum(top, jnp.max(s.reshape(chunk // 8, 8, queries), axis=0))

    def low():
        return jnp.full((8, queries), -jnp.inf, f32)

    def step(head, slot, peak, more):
        if before is None:
            mixed = jnp.zeros((2 * HEAD, queries), f32)
        else:
            earlier, mixed = before(head)
            peak = jnp.maximum(peak, earlier)
            mixed = mixed * jnp.exp(earlier - peak)
        top = low()
        q_next = of_head(head + 1) if more else None
        for c in range(keys // chunk):
            if more:
                top = score(q_next, 1 - slot, c, top)
            p = jnp.exp(s_ref[slot, c * chunk : (c + 1) * chunk, :] - peak).astype(bf16)
            mixed = mixed + dot(vt_ref[head, :, c * chunk : (c + 1) * chunk], p)
        finish(head, peak, mixed)
        return jnp.max(top, axis=0, keepdims=True)

    top = low()
    q_first = of_head(0)
    for c in range(keys // chunk):
        top = score(q_first, 0, c, top)
    peak = jnp.max(top, axis=0, keepdims=True)

    def pair(i, peak):
        peak = step(2 * i, 0, peak, True)
        return step(2 * i + 1, 1, peak, True)

    peak = lax.fori_loop(0, heads // 2 - 1, pair, peak)
    peak = step(heads - 2, 0, peak, True)
    step(heads - 1, 1, peak, False)


def divide(at_ref):
    def finish(head, peak, mixed):
        at_ref[head] = (mixed[:HEAD] / mixed[HEAD:]).astype(bf16)

    return finish


def joined(at_ref):
    heads, size, queries = at_ref.shape
    return jnp.transpose(at_ref[...].reshape(heads * size, queries))


def attend_scratch(heads, queries, keys):
    width = heads * HEAD
    return [
        pltpu.VMEM((keys, width), bf16),
        pltpu.VMEM((heads, 2 * HEAD, keys), bf16),
        pltpu.VMEM((2, keys, queries), f32),
    ]


def load_values(vt_ref, values, heads):
    keys = values.shape[0]
    vt_ref[:, :HEAD, :] = jnp.transpose(values).reshape(heads, HEAD, keys)
    vt_ref[:, HEAD:, :] = jnp.ones((heads, HEAD, keys), bf16)


SCALE = 1.0 / math.sqrt(HEAD)


def own_kernel(own_ref, qkv_ref, qt_ref, peak_ref, mixed_ref, k, vt, s):
    own = own_ref[...]
    qt_ref[...] = jnp.transpose(dot(own, qkv_ref[0]).astype(bf16) * bf16(SCALE))
    k[...] = dot(own, qkv_ref[1]).astype(bf16)
    load_values(vt, dot(own, qkv_ref[2]).astype(bf16), H4)

    def finish(head, peak, mixed):
        peak_ref[head] = peak
        mixed_ref[head] = mixed

    attend(H4, k, qt_ref, vt, s, finish)


def other_kernel(
    other_ref,
    qkv_ref,
    qt_ref,
    peak_ref,
    mixed_ref,
    rows_ref,
    proj_ref,
    weight_ref,
    child_ref,
    out_ref,
    parts_ref,
    k,
    vt,
    s,
    at,
):
    other = other_ref[...]
    k[...] = dot(other, qkv_ref[1]).astype(bf16)
    load_values(vt, dot(other, qkv_ref[2]).astype(bf16), H4)
    attend(H4, k, qt_ref, vt, s, divide(at), lambda head: (peak_ref[head], mixed_ref[head]))
    fine = (rows_ref[...].astype(f32) + dot(joined(at), proj_ref[...])).astype(bf16)
    out_ref[...] = fine
    pool_own(fine, weight_ref, child_ref, parts_ref)


def coarse_kernel(q_ref, both_ref, proj_ref, out_ref, k, vt, s, qt, at):
    n, width = q_ref.shape
    qt[...] = jnp.transpose(q_ref[...] * bf16(SCALE))
    k[...] = both_ref[:, :width]
    values = both_ref[:, width:]
    load_values(vt, values, width // HEAD)
    attend(width // HEAD, k, qt, vt, s, divide(at))
    terms = dot(joined(at), proj_ref[...]).astype(bf16)
    parts = out_ref.shape[0]
    for g in range(parts):
        out_ref[g] = terms[:, g * width : (g + 1) * width]


EDGE = 16


def gelu(values):
    return jax.nn.gelu(values, approximate=True).astype(bf16)


def three_terms(value):
    first = value.astype(bf16).astype(f32)
    second = (value - first).astype(bf16).astype(f32)
    return [first, second, value - first - second]


def run_starts(child_ref, n):
    nx = lax.axis_size("x")
    return child_ref[0:1, :] - lax.axis_index(PTS) * (nx * n)


def pool_own(fine, weight_ref, child_ref, parts_ref):
    n = fine.shape[0]
    points = child_ref.shape[1]
    groups, _, width = parts_ref.shape
    start_row = run_starts(child_ref, n) - lax.axis_index("x") * n
    start = column(start_row)
    rows = lax.broadcasted_iota(jnp.int32, (n, points), 0)
    first = jnp.where(start_row == rows, 1.0, 0.0).astype(bf16)
    opens = dot(first, jnp.ones((points, width), bf16))
    place = one_hot(start, n)
    last = jnp.max(
        jnp.where(start_row < n, start_row.astype(f32), -1.0), axis=1, keepdims=True
    ).astype(jnp.int32)
    tail = KIDS
    leaving = lax.broadcasted_iota(jnp.int32, (tail, width), 0) + (n - tail) >= last
    edge_row = lax.broadcasted_iota(jnp.int32, (EDGE, width), 0)

    def ahead(block, k):
        return jnp.concatenate([block[k:], jnp.ones((k, width), f32)], axis=0)

    cut = ahead(opens, 1)
    cuts = []
    reach = 1
    while reach < KIDS:
        cuts.append((reach, cut > 0.0))
        cut = jnp.maximum(cut, ahead(cut, reach))
        reach *= 2
    for g in range(groups):
        best = dot(fine, weight_ref[:, g * width : (g + 1) * width])
        lifted_tail = best[n - tail :]
        for reach, ends in cuts:
            best = jnp.where(ends, best, jnp.maximum(best, ahead(best, reach)))
        parts_ref[g, :points, :] = dot(place, gelu(best)).astype(bf16)
        head = jnp.max(jnp.where(leaving, lifted_tail, -jnp.inf), axis=0, keepdims=True)
        edge = jnp.zeros((EDGE, width), f32)
        for at, value in ((0, head), (8, best[0:1])):
            for i, term in enumerate(three_terms(value)):
                edge = jnp.where(edge_row == at + i, term, edge)
        parts_ref[g, points:, :] = edge.astype(bf16)


def pool_kernel(parts_ref, child_ref, asked_ref, out_ref):
    groups = parts_ref.shape[0]
    points = child_ref.shape[1]
    n, width = out_ref.shape
    start_row = run_starts(child_ref, n)
    point = lax.broadcasted_iota(jnp.int32, (points, width), 0)
    pooled = parts_ref[0, :points, :].astype(f32)
    for g in range(1, groups):
        pooled = pooled + parts_ref[g, :points, :].astype(f32)

    def edge(g, at):
        block = parts_ref[g, points:, :].astype(f32)
        return block[at : at + 1] + block[at + 1 : at + 2] + block[at + 2 : at + 3]

    def count(hits):
        return jnp.sum(jnp.where(hits, 1.0, 0.0), axis=1, keepdims=True).astype(jnp.int32)

    for g in range(1, groups):
        whole = gelu(jnp.maximum(edge(g - 1, 0), edge(g, 8))).astype(f32)
        crossing = count(start_row < g * n) - 1
        crossing = jnp.where(count(start_row == g * n) > 0, -1, crossing)
        pooled = jnp.where(point == crossing, whole, pooled)
    out_ref[...] = dot(pick_of(asked_ref, 1, points), pooled.astype(bf16)).astype(bf16)


def norm5_kernel(
    slot_ref, parts_ref, gain_hbm, qkv_ref, q_ref, kv_ref, cols_ref, gain, sems
):
    copies = fetch([(gain_hbm, gain)], sems)
    n = slot_ref.shape[1]
    groups, width = parts_ref.shape[1], parts_ref.shape[3]
    pick = one_hot(column(slot_ref[...]), n)
    parts = [parts_ref[:, g].reshape(n, width) for g in range(groups)]
    own = parts_ref[:, pl.ds(lax.axis_index("x"), 1)].reshape(n, width)
    picked = dot(pick, jnp.concatenate(parts + [own], axis=1)).astype(bf16)
    rows = picked[:, : groups * width]
    cols_ref[...] = picked[:, groups * width :]
    copies[0].wait()
    normed = layer_norm(rows, gain[...])
    q_ref[...] = dot(normed, qkv_ref[0]).astype(bf16)
    kv_ref[:, :width] = dot(normed, qkv_ref[1]).astype(bf16)
    kv_ref[:, width:] = dot(normed, qkv_ref[2]).astype(bf16)


def sum_kernel(cols_ref, parts_ref, out_ref):
    total = cols_ref[...].astype(f32)
    summed = parts_ref[0].astype(f32)
    for g in range(1, parts_ref.shape[0]):
        summed = summed + parts_ref[g].astype(f32)
    out_ref[...] = (total + summed).astype(bf16)


def shape(dims, dtype=bf16):
    return jax.ShapeDtypeStruct(dims, dtype)


def exchange(block, axes):
    return lax.all_to_all(block, axes, split_axis=0, concat_axis=0, tiled=True)


VMEM = pl.BlockSpec(memory_space=pltpu.VMEM)
HBM = pl.BlockSpec(memory_space=pltpu.HBM)
DMA = pltpu.SemaphoreType.DMA


def kernel(body, name, out_shape, scratch=(), in_specs=None, flops=0):
    extra = {} if in_specs is None else {"in_specs": in_specs}
    if flops:
        extra["cost_estimate"] = pl.CostEstimate(
            flops=flops, bytes_accessed=1 << 20, transcendentals=0
        )
    return pl.pallas_call(
        body,
        out_shape=out_shape,
        scratch_shapes=list(scratch),
        compiler_params=pltpu.CompilerParams(vmem_limit_bytes=48 << 20),
        name=name,
        **extra,
    )


def local(
    feats4, order4, gain4, qkv4, proj4, pool_weight, child5, mask5, order5, gain5, qkv5, proj5
):
    n = feats4.shape[0]
    nz = lax.axis_size("z")
    planes = lax.axis_size("y") * lax.axis_size("c") * lax.axis_size("x")
    nx = lax.axis_size("x")
    pts_count = nz * planes // nx

    wanted, owner4, slot5 = kernel(
        functools.partial(request_kernel, planes),
        "request",
        [shape((nz, 2, planes), jnp.int32), shape((1, n), jnp.int32), shape((1, n), jnp.int32)],
        [pltpu.VMEM((1, n), jnp.int32), pltpu.VMEM((1, n), jnp.int32), DMA((2,))],
        [HBM, HBM],
    )(order4.reshape(1, n), order5.reshape(1, n))
    asked = exchange(exchange(wanted, ("z",)).transpose(2, 1, 0), PLANE)

    outgoing = kernel(pick_kernel, "pick4", shape((n, C4)))(asked, feats4)
    arrived = exchange(outgoing.reshape(n, 2, C4 // 2), ALL).reshape(n, C4)
    curve_rows, normed4 = kernel(
        norm4_kernel,
        "norm4",
        [shape((n, C4)), shape((n, C4))],
        [pltpu.VMEM((1, C4), f32), DMA((1,))],
        [VMEM, VMEM, HBM],
    )(owner4, arrived, gain4.reshape(1, C4))
    other4 = lax.ppermute(normed4, "x", [(i, i ^ 1) for i in range(nx)])
    half = 4 * n * n * C4 * H4
    qt4, peak4, mixed4 = kernel(
        own_kernel,
        "attend4_own",
        [shape((C4, n)), shape((H4, 1, n), f32), shape((H4, 2 * HEAD, n), f32)],
        attend_scratch(H4, n, n),
        flops=half,
    )(normed4, qkv4)
    child_rows = child5.T
    width = C5 // nx
    fine_out, parts4 = kernel(
        other_kernel,
        "attend4_other",
        [shape((n, C4)), shape((nx, n + EDGE, width))],
        attend_scratch(H4, n, n) + [pltpu.VMEM((H4, HEAD, n), bf16)],
        flops=half,
    )(other4, qkv4, qt4, peak4, mixed4, curve_rows, proj4, pool_weight, child_rows)

    pooled = kernel(pool_kernel, "pool", shape((n, width)))(
        exchange(parts4, "x"), child_rows, asked
    )
    by_z = exchange(pooled.reshape(nz, n // nz, width), ("z",))
    by_z = by_z.reshape(nz, planes // nx, n // pts_count, width).transpose(1, 0, 2, 3)
    copies = jnp.broadcast_to(
        by_z.reshape(planes // nx, 1, n * nx // planes, width),
        (planes // nx, nx, n * nx // planes, width),
    )
    parts5 = exchange(copies.reshape(planes, n * nx // planes, width), PLANE)
    parts5 = parts5.reshape(copies.shape)
    query5, kv5, own_columns = kernel(
        norm5_kernel,
        "norm5",
        [shape((n, width)), shape((n, 2 * width)), shape((n, width))],
        [pltpu.VMEM((1, C5), f32), DMA((1,))],
        [VMEM, VMEM, HBM, VMEM],
    )(slot5, parts5, gain5.reshape(1, C5), qkv5)
    both5 = lax.all_gather(kv5, "c", axis=0, tiled=True)
    terms = kernel(
        coarse_kernel,
        "attend5",
        shape((nx, n, width)),
        attend_scratch(width // HEAD, n, 2 * n)
        + [pltpu.VMEM((width, n), bf16), pltpu.VMEM((width // HEAD, HEAD, n), bf16)],
    )(query5, both5, proj5)
    coarse_out = kernel(sum_kernel, "add5", shape((n, width)))(own_columns, exchange(terms, "x"))
    return (fine_out, coarse_out)


def solution(mesh):
    pts, grp = mesh.devices.shape
    inner = Mesh(mesh.devices.reshape(pts // 8, 4, 2, grp), ALL)
    in_specs = (
        P(ALL, None),
        P(ALL),
        P(),
        P(),
        P(),
        P(),
        P(PTS, None),
        P(PTS, None),
        P(PTS),
        P(),
        P(None, None, "x"),
        P("x", None),
    )
    out_specs = (P(ALL, None), P(PTS, "x"))
    return jax.shard_map(local, mesh=inner, in_specs=in_specs, out_specs=out_specs, check_vma=False)
```

time: 188 us -> 170 us (0.904)
  waiting for transfers between devices: 23.1 us -> 1.28 us
  blocking collectives: 123 us -> 136 us
  starting transfers between devices: 8.89 us -> 2.37 us
  local copies, waits for them, and re-layouts: 6.14 us -> 4.21 us
    all_to_all x1 -> x0, waiting for transfers between devices: 14.8 us -> none  [exchange(): return lax.all_to_all(block, axes, split_axis=0, concat_axis=0, tiled=True)]
    all_to_all x6 -> x7, blocking collectives: 123 us -> 134 us  [exchange(): return lax.all_to_all(block, axes, split_axis=0, concat_axis=0, tiled=True)]
    ppermute x1, waiting for transfers between devices: 7.1 us -> 1.28 us  [local(): other4 = lax.ppermute(normed4, 'x', [(i, i ^ 1) for i in range(nx)])]
    all_to_all x1 -> x0, starting transfers between devices: 3.51 us -> none  [exchange(): return lax.all_to_all(block, axes, split_axis=0, concat_axis=0, tiled=True)]
    ppermute x1 -> x0, starting transfers between devices: 3.14 us -> none  [local(): other5 = lax.ppermute(kv5, 'c', [(0, 1), (1, 0)])]
    all_gather x0 -> x1, blocking collectives: none -> 2.5 us  [local(): both5 = lax.all_gather(kv5, 'c', axis=0, tiled=True)]
    broadcast_in_dim x2, local copies, waits for them, and re-layouts: 2.06 us -> 0.13 us  [local(): jnp.broadcast_to(by_z.reshape(planes // nx, 1, n * nx // planes, width),...]
    pallas_call x8 -> x9, Pallas kernels: 24.1 us -> 25.1 us  [the longest x1 7.91 us: local(): kernel(other_kernel, 'attend4_other', [shape((n, C4)), shape((nx, n + EDG...]
  transfers between devices with their start and end apart: 3 -> 1, of which waited for: 3 -> 1; matrix products, arithmetic and copies ran while one was open for 0% -> 0% of each run, Pallas kernels for 0% -> 3%
where the time goes in v2:
time: 170 us
  blocking collectives  136 us (80%)
  Pallas kernels  25.1 us (15%)
  local copies, waits for them, and re-layouts  4.21 us (2%)
  starting transfers between devices  2.37 us (1%)
    all_to_all x7, blocking collectives, exchange(): return lax.all_to_all(block, axes, split_axis=0, concat_axis=0, tiled=True)  134 us
    pallas_call x1, Pallas kernels, local(): kernel(other_kernel, 'attend4_other', [shape((n, C4)), shape((nx, n + EDG...  7.91 us
    pallas_call x1, Pallas kernels, local(): kernel(own_kernel, 'attend4_own', [shape((C4, n)), shape((H4, 1, n), f32)...  5.81 us
    pallas_call x1, Pallas kernels, local(): kernel(coarse_kernel, 'attend5', shape((nx, n, width)), attend_scratch(wi...  5.07 us
    unnamed x23, local copies, waits for them, and re-layouts  3.77 us
  transfers between devices with their start and end apart: 1, of which 1 were waited for; matrix products, arithmetic and copies ran while one was open for 0% of the time, Pallas kernels for 3%

profile of v2, /device:TPU:1, one launch (start us, length us, event | category | flops | bytes accessed | tf_op | source)
XLA Modules:
  0.0 169.9 jit_solution(11257887980273046769)
XLA Ops:
  0.6 0.7 copy-done.5
  1.3 0.7 copy-done.6
  2.0 1.2 request.1
  3.2 26.9 %all_to_all.35 = s32[16,2,32]{2,1,0:T(2,128)S(1)} all-to-all(s32[16,2,32]{2,1,0:T(2,128)S(1)} %get-tuple-element.16), channel_id=1, replica_groups=mesh['z'=16,'y'=4,'c'=2,'x'=4] {'z'}, dimensions={0} | all-to-all | bytes 8192 | tf_op jit(solution)/shard_map/all_to_all | solution.py:354
  30.2 0.1 copy.20
  30.3 16.2 %all_to_all.36.asked_ref = s32[32,2,16]{2,1,0:T(2,128)S(1)} all-to-all(s32[32,2,16]{2,1,0:T(2,128)S(1)} %bitcast.30), channel_id=1, replica_groups=mesh['z'=16,'y'=4,'c'=2,'x'=4] {'y','c','x'}, dimensions={0} | all-to-all | bytes 8192 | tf_op jit(solution)/shard_map/all_to_all | solution.py:354
  46.4 0.9 copy-done.1
  47.4 0.7 pick4.1
  48.1 0.1 reshape.38
  48.2 34.1 %all_to_all.37 = bf16[512,2,128]{2,1,0:T(2,128)(2,1)S(1)} all-to-all(bf16[512,2,128]{2,1,0:T(2,128)(2,1)S(1)} %reshape.38), channel_id=1, replica_groups=mesh['z'=16,'y'=4,'c'=2,'x'=4] {'z','y','c','x'}, dimensions={0} | all-to-all | bytes 524288 | tf_op jit(solution)/shard_map/all_to_all | solution.py:354
  82.3 0.7 copy-done.7
  83.1 0.8 norm4.1
  83.9 0.0 copy-start.3
  83.9 0.0 copy-start.9
  83.9 2.4 %collective-permute-start = (bf16[512,256]{1,0:T(8,128)(2,1)S(1)}, bf16[512,256]{1,0:T(8,128)(2,1)S(1)}, u32[]{:S(2)}, u32[]{:S(2)}) collective-permute-start(bf16[512,256]{1,0:T(8,128)(2,1)S(1)} %get-tuple-element.17.own_ref), channel_id=1, source_target_pairs={{0,1},{1,0},{2,3},{3,2},{4,5},{5,4},{6,7},{7,6},{8,9},{9,8},{10,11... | collective-permute-start | bytes 786440 | tf_op jit(solution)/shard_map/ppermute | solution.py:405
  86.3 5.8 %attend4_own.1 = (bf16[256,512]{1,0:T(8,128)(2,1)S(1)}, f32[16,1,512]{2,1,0:T(1,128)S(1)}, f32[16,32,512]{2,1,0:T(8,128)S(1)}) custom-call(bf16[512,256]{1,0:T(8,128)(2,1)S(1)} %get-tuple-element.17.own_ref, bf16[3,256,256]{2,1,0:T(8,128)(2,1)S(1)} %copy-done.8), custom_call_target="tpu_custom_call" | custom-call | flops 4294967296 | bytes 1048576 | tf_op jit(solution)/shard_map/attend4_own/pallas_call | solution.py:407
  92.1 1.3 collective-permute-done.other_ref
  93.4 7.9 %attend4_other.1 = (bf16[512,256]{1,0:T(8,128)(2,1)}, bf16[4,528,128]{2,1,0:T(8,128)(2,1)S(1)}) custom-call(bf16[512,256]{1,0:T(8,128)(2,1)S(1)} %collective-permute-done.other_ref, bf16[3,256,256]{2,1,0:T(8,128)(2,1)S(1)} %copy-done.8, bf16[256,512]{1,0:T(8,128)(2,1)S(1)} %get-tuple-element.18.qt_ref, f32[16,1,512]{2,1,0:T(1,128)S(1)} %get-tuple-element.19.peak_ref, ...), custom_call_target="tpu_custom_call" | custom-call | flops 4294967296 | bytes 1048576 | tf_op jit(solution)/shard_map/attend4_other/pallas_call | solution.py:416
  101.3 11.1 %all_to_all.38.parts_ref = bf16[4,528,128]{2,1,0:T(8,128)(2,1)S(1)} all-to-all(bf16[4,528,128]{2,1,0:T(8,128)(2,1)S(1)} %get-tuple-element.24), channel_id=1, replica_groups=mesh['z'=16,'y'=4,'c'=2,'x'=4] {'x'}, dimensions={0} | all-to-all | bytes 1081344 | tf_op jit(solution)/shard_map/all_to_all | solution.py:354
  112.4 0.8 pool.1
  113.2 14.7 %all_to_all.39 = bf16[16,32,128]{2,1,0:T(8,128)(2,1)S(1)} all-to-all(bf16[16,32,128]{2,1,0:T(8,128)(2,1)S(1)} %bitcast.19), channel_id=1, replica_groups=mesh['z'=16,'y'=4,'c'=2,'x'=4] {'z'}, dimensions={0} | all-to-all | bytes 262144 | tf_op jit(solution)/shard_map/all_to_all | solution.py:354
  127.9 0.1 copy.21
  128.0 0.1 copy.22
  128.1 0.1 broadcast_in_dim.8
  128.2 19.2 %all_to_all.40 = bf16[32,64,128]{2,1,0:T(8,128)(2,1)S(1)} all-to-all(bf16[32,64,128]{2,1,0:T(8,128)(2,1)S(1)} %bitcast.26), channel_id=1, replica_groups=mesh['z'=16,'y'=4,'c'=2,'x'=4] {'y','c','x'}, dimensions={0} | all-to-all | bytes 1048576 | tf_op jit(solution)/shard_map/all_to_all | solution.py:354
  147.4 0.7 copy-done.4
  148.1 2.0 %norm5.1 = (bf16[512,128]{1,0:T(8,128)(2,1)S(1)}, bf16[512,256]{1,0:T(8,128)(2,1)S(1)}, bf16[512,128]{1,0:T(8,128)(2,1)S(1)}) custom-call(s32[1,512]{1,0:T(1,128)S(1)} %get-tuple-element.23.slot_ref, bf16[8,4,64,128]{3,2,1,0:T(8,128)(2,1)S(1)} %bitcast.17, f32[1,512]{1,0:T(1,128)S(1)} %bitcast.22, bf16[3,512,128]{2,1,0:T(8,128)(2,1)S(1)} %copy-done), custom_call_target="tpu_custom_call" | custom-call | tf_op jit(solution)/shard_map/norm5/pallas_call | solution.py:435
  150.0 0.0 copy-start.2
  150.0 2.5 %all_gather.3.both_ref = bf16[1024,256]{1,0:T(8,128)(2,1)S(1)} all-gather(bf16[512,256]{1,0:T(8,128)(2,1)S(1)} %get-tuple-element.27), channel_id=1, replica_groups=mesh['z'=16,'y'=4,'c'=2,'x'=4] {'c'}, dimensions={0}, use_global_device_ids=true | all-gather | bytes 786432 | tf_op jit(solution)/shard_map/all_gather | solution.py:442
  152.6 5.1 %attend5.1 = bf16[4,512,128]{2,1,0:T(8,128)(2,1)S(1)} custom-call(bf16[512,128]{1,0:T(8,128)(2,1)S(1)} %get-tuple-element.26.q_ref, bf16[1024,256]{1,0:T(8,128)(2,1)S(1)} %all_gather.3.both_ref, bf16[128,512]{1,0:T(8,128)(2,1)S(1)} %copy-done.2), custom_call_target="tpu_custom_call" | custom-call | tf_op jit(solution)/shard_map/attend5/pallas_call | solution.py:443
  157.6 11.6 %all_to_all.41.parts_ref = bf16[4,512,128]{2,1,0:T(8,128)(2,1)S(1)} all-to-all(bf16[4,512,128]{2,1,0:T(8,128)(2,1)S(1)} %attend5.1), channel_id=1, replica_groups=mesh['z'=16,'y'=4,'c'=2,'x'=4] {'x'}, dimensions={0} | all-to-all | bytes 1048576 | tf_op jit(solution)/shard_map/all_to_all | solution.py:354
  169.2 0.7 add5.1
  (16 shorter events, 0.1 us)
Async XLA Ops:
  0.6 0.7 copy-start.5
  1.3 0.7 copy-start.6
  46.4 1.0 copy-start.1
  82.3 4.0 %copy-start.8 = (bf16[3,256,256]{2,1,0:T(8,128)(2,1)S(1)}, bf16[3,256,256]{2,1,0:T(8,128)(2,1)}, u32[]{:S(2)}) copy-start(bf16[3,256,256]{2,1,0:T(8,128)(2,1)} %qkv_ref.4) | copy-start | bytes 1179652
  82.3 0.7 copy-start.7
  83.9 9.5 %copy-start.3 = (s32[512,8]{0,1:T(8,128)S(1)}, s32[512,8]{0,1:T(8,128)}, u32[]{:S(2)}) copy-start(s32[512,8]{0,1:T(8,128)} %param.18) | copy-start | bytes 49156
  83.9 9.5 %copy-start.9 = (bf16[256,512]{1,0:T(8,128)(2,1)S(1)}, bf16[256,512]{1,0:T(8,128)(2,1)}, u32[]{:S(2)}) copy-start(bf16[256,512]{1,0:T(8,128)(2,1)} %weight_ref.1) | copy-start | bytes 786436
  83.9 9.5 %copy-start.10 = (bf16[256,256]{1,0:T(8,128)(2,1)S(1)}, bf16[256,256]{1,0:T(8,128)(2,1)}, u32[]{:S(2)}) copy-start(bf16[256,256]{1,0:T(8,128)(2,1)} %proj_ref.2) | copy-start | bytes 393220
  83.9 9.5 %collective-permute-start = (bf16[512,256]{1,0:T(8,128)(2,1)S(1)}, bf16[512,256]{1,0:T(8,128)(2,1)S(1)}, u32[]{:S(2)}, u32[]{:S(2)}) collective-permute-start(bf16[512,256]{1,0:T(8,128)(2,1)S(1)} %get-tuple-element.17.own_ref), channel_id=1, source_target_pairs={{0,1},{1,0},{2,3},{3,2},{4,5},{5,4},{6,7},{7,6},{8,9},{9,8},{10,11... | collective-permute-start | bytes 786440 | tf_op jit(solution)/shard_map/ppermute | solution.py:405
  128.2 19.2 %copy-start = (bf16[3,512,128]{2,1,0:T(8,128)(2,1)S(1)}, bf16[3,512,128]{2,1,0:T(8,128)(2,1)}, u32[]{:S(2)}) copy-start(bf16[3,512,128]{2,1,0:T(8,128)(2,1)} %qkv_ref.5) | copy-start | bytes 1179652
  147.4 0.7 copy-start.4
  150.0 2.5 %copy-start.2 = (bf16[128,512]{1,0:T(8,128)(2,1)S(1)}, bf16[128,512]{1,0:T(8,128)(2,1)}, u32[]{:S(2)}) copy-start(bf16[128,512]{1,0:T(8,128)(2,1)} %proj_ref.3) | copy-start | bytes 393220

commit v3 on v2

v3 whole, which is shorter than its diff:
```python
import functools
import math

import jax
import jax.numpy as jnp
from jax import lax
from jax.experimental import pallas as pl
from jax.experimental.pallas import tpu as pltpu
from jax.sharding import Mesh
from jax.sharding import PartitionSpec as P

C4 = 256
H4 = 16
C5 = 512
H5 = 32
HEAD = 16
KIDS = 8

epsilon = 1e-05
f32 = jnp.float32
bf16 = jnp.bfloat16

PTS = ("z", "y", "c")
PLANE = ("y", "c", "x")
CHIPS = ("z", "y", "x")
ALL = ("z", "y", "c", "x")


def dot(a, b):
    return jnp.dot(a, b, preferred_element_type=f32)


def column(row):
    return jnp.transpose(jnp.broadcast_to(row, (8, row.shape[1])))[:, :1]


def columns(*rows):
    n = rows[0].shape[1]
    fill = [jnp.zeros((8 - len(rows), n), jnp.int32)] if len(rows) < 8 else []
    block = jnp.transpose(jnp.concatenate(list(rows) + fill, axis=0))
    return [block[:, i : i + 1] for i in range(len(rows))]


def one_hot(col, width):
    lanes = lax.broadcasted_iota(jnp.int32, (col.shape[0], width), 1)
    return jnp.where(col == lanes, 1.0, 0.0).astype(bf16)


def layer_norm(rows_in, norm_gain):
    values = rows_in.astype(f32)
    center = values - jnp.mean(values, axis=-1, keepdims=True)
    spread = jnp.mean(center * center, axis=-1, keepdims=True)
    return (center * lax.rsqrt(spread + epsilon) * norm_gain).astype(bf16)


def fetch(pairs, sems):
    copies = [pltpu.make_async_copy(a, b, sems.at[i]) for i, (a, b) in enumerate(pairs)]
    for copy in copies:
        copy.start()
    return copies


def request_kernel(planes, orders_ref, out_ref, owner_ref, slot_ref):
    o4, o5 = orders_ref[0:1, :], orders_ref[1:2, :]
    n = o4.shape[1]
    nz, nx = out_ref.shape[0], lax.axis_size("x")
    x = lax.axis_index("x")
    owner4, owner5 = o4 // n, o5 // n
    ny, half, per_z = planes // (2 * nx), planes // 2, planes // nx
    u = owner4 % planes
    lane4 = u // nx % 2 * half + u // (2 * nx) * nx + u % nx
    owner_ref[...] = u // nx % 2 * (n // 2) + owner4 // planes * half + lane4 % half
    of_pts = owner5 % per_z
    pair5 = of_pts % 2 * ny + of_pts // 2
    lane4_col, row4_col, owner5_col, pair5_col, row5_col = columns(
        lane4, o4 % n, owner5, pair5, o5 % n
    )

    lanes = lax.broadcasted_iota(jnp.int32, (n, n), 1)
    rows = lax.broadcasted_iota(jnp.int32, (n, n), 0)
    earlier = jnp.where((owner5_col == owner5) & (rows < lanes), 1.0, 0.0)
    rank = jnp.sum(earlier, axis=0, keepdims=True).astype(jnp.int32)
    slot_ref[...] = ((owner5 % per_z) * nz + owner5 // per_z) * nx + rank

    lane = lax.broadcasted_iota(jnp.int32, (n, planes), 1)
    zs = lax.broadcasted_iota(jnp.int32, (nz, n), 0)

    def table(z_hit, u_hit, row):
        low = jnp.where(u_hit, (row % 256).astype(f32), 0.0)
        high = jnp.where(u_hit, (row // 256).astype(f32), 0.0)
        both = dot(
            jnp.where(z_hit, 1.0, 0.0).astype(bf16),
            jnp.concatenate([low, high], axis=1).astype(bf16),
        )
        return (both[:, :planes] + 256.0 * both[:, planes:]).astype(jnp.int32)

    want4 = table(zs == owner4 // planes, lane4_col == lane, row4_col)
    own_rank = (zs == owner5 // per_z) & (rank == x)
    want5 = table(own_rank, pair5_col == lane // nx, row5_col)
    for c in range(2):
        out_ref[:, c, :] = want4[:, c * half : (c + 1) * half]
        out_ref[:, 2 + c, :] = want5[:, c * half : (c + 1) * half]


def picks(cols, width):
    return jnp.concatenate([one_hot(cols[:, i : i + 1], width) for i in range(cols.shape[1])], axis=0)


def pick_kernel(asked_ref, table_ref, out_ref):
    nz = asked_ref.shape[1] // 4
    n, width = table_ref.shape[0] // 2, table_ref.shape[1]
    for c in range(2):
        pick = picks(asked_ref[:, c * nz : (c + 1) * nz], n)
        out_ref[:, c * width : (c + 1) * width] = dot(
            pick, table_ref[c * n : (c + 1) * n, :]
        ).astype(bf16)


def prepare_kernel(
    owner_ref,
    slot_ref,
    asked_ref,
    child_ref,
    gain_ref,
    pick4_ref,
    pick5_ref,
    want5_ref,
    place_ref,
    ends_ref,
    gain_out_ref,
):
    gain_out_ref[...] = gain_ref[...]
    n = owner_ref.shape[1]
    points = child_ref.shape[1]
    pick4_ref[...] = one_hot(column(owner_ref[...]), n)
    pick5_ref[...] = one_hot(column(slot_ref[...]), n)

    start_row = run_starts(child_ref, n)
    room = place_ref.shape[0]
    at = lax.broadcasted_iota(jnp.int32, (1, points), 1)
    for g in range(want5_ref.shape[1] // room):
        before = count(start_row < g * n)
        at = jnp.where(start_row // n == g, at - before + g * room, at)
    nz = asked_ref.shape[1] // 4
    asked5 = jnp.where(
        lax.axis_index("c") == 0, asked_ref[:, 2 * nz : 3 * nz], asked_ref[:, 3 * nz :]
    )
    wanted = picks(asked5, points).astype(f32)
    spot = jnp.sum(wanted * at.astype(f32), axis=1, keepdims=True).astype(jnp.int32)
    want5_ref[...] = one_hot(spot, want5_ref.shape[1])

    own_row = own_starts(child_ref, n)
    own = column(own_row)
    lanes = lax.broadcasted_iota(jnp.int32, (points, n), 1)
    opened = jnp.where((own >= 0) & (own <= lanes), 1.0, 0.0)
    number = jnp.sum(opened, axis=0, keepdims=True).astype(jnp.int32) - 1
    opens_here = jnp.sum(jnp.where(own == lanes, 1.0, 0.0), axis=0, keepdims=True)
    spots = lax.broadcasted_iota(jnp.int32, (room, n), 0)
    place_ref[...] = jnp.where((spots == number) & (opens_here > 0.0), 1.0, 0.0).astype(bf16)

    rows = lax.broadcasted_iota(jnp.int32, (n, points), 0)
    first = jnp.where(own_row == rows, 1.0, 0.0).astype(bf16)
    opens = dot(first, jnp.ones((points, ends_ref.shape[2]), bf16))
    cut = ahead(opens, 1, 1.0)
    for i in range(ends_ref.shape[0]):
        ends_ref[i] = cut
        cut = jnp.maximum(cut, ahead(cut, 1 << i, 1.0))


def norm4_kernel(pick_ref, arrived_ref, gain_ref, rows_ref, normed_ref):
    width = rows_ref.shape[1]
    arrived = jnp.concatenate([arrived_ref[:, :width], arrived_ref[:, width:]], axis=0)
    rows = dot(pick_ref[...], arrived).astype(bf16)
    rows_ref[...] = rows
    normed_ref[...] = layer_norm(rows, gain_ref[...])


def attend(heads, k_ref, qt_ref, vt_ref, s_ref, finish, before=None, chunk=512):
    width = heads * HEAD
    queries = qt_ref.shape[1]
    keys = k_ref.shape[0]
    row_head = lax.broadcasted_iota(jnp.int32, (width, queries), 0) // HEAD

    def of_head(head):
        q = qt_ref[...]
        return jnp.where(row_head == head, q, jnp.zeros_like(q))

    def score(q_head, slot, c, top):
        s = dot(k_ref[c * chunk : (c + 1) * chunk, :], q_head)
        s_ref[slot, c * chunk : (c + 1) * chunk, :] = s
        return jnp.maximum(top, jnp.max(s.reshape(chunk // 8, 8, queries), axis=0))

    def low():
        return jnp.full((8, queries), -jnp.inf, f32)

    def step(head, slot, peak, more):
        if before is None:
            mixed = jnp.zeros((2 * HEAD, queries), f32)
        else:
            earlier, mixed = before(head)
            peak = jnp.maximum(peak, earlier)
            mixed = mixed * jnp.exp(earlier - peak)
        top = low()
        q_next = of_head(head + 1) if more else None
        for c in range(keys // chunk):
            if more:
                top = score(q_next, 1 - slot, c, top)
            p = jnp.exp(s_ref[slot, c * chunk : (c + 1) * chunk, :] - peak).astype(bf16)
            mixed = mixed + dot(vt_ref[head, :, c * chunk : (c + 1) * chunk], p)
        finish(head, peak, mixed)
        return jnp.max(top, axis=0, keepdims=True)

    top = low()
    q_first = of_head(0)
    for c in range(keys // chunk):
        top = score(q_first, 0, c, top)
    peak = jnp.max(top, axis=0, keepdims=True)

    def pair(i, peak):
        peak = step(2 * i, 0, peak, True)
        return step(2 * i + 1, 1, peak, True)

    peak = lax.fori_loop(0, heads // 2 - 1, pair, peak)
    peak = step(heads - 2, 0, peak, True)
    step(heads - 1, 1, peak, False)


def divide(at_ref):
    def finish(head, peak, mixed):
        at_ref[head] = (mixed[:HEAD] / mixed[HEAD:]).astype(bf16)

    return finish


def joined(at_ref):
    heads, size, queries = at_ref.shape
    return jnp.transpose(at_ref[...].reshape(heads * size, queries))


def attend_scratch(heads, queries, keys):
    width = heads * HEAD
    return [
        pltpu.VMEM((keys, width), bf16),
        pltpu.VMEM((heads, 2 * HEAD, keys), bf16),
        pltpu.VMEM((2, keys, queries), f32),
    ]


def load_values(vt_ref, values, heads):
    keys = values.shape[1]
    vt_ref[:, :HEAD, :] = values.reshape(heads, HEAD, keys)
    vt_ref[:, HEAD:, :] = jnp.ones((heads, HEAD, keys), bf16)


SCALE = 1.0 / math.sqrt(HEAD)


def across(weights, rows):
    return lax.dot_general(weights, rows, (((0,), (1,)), ((), ())), preferred_element_type=f32)


def own_kernel(
    own_ref, qkv_ref, gain_ref, qt_ref, peak_ref, mixed_ref, gain_out_ref, k, vt, s
):
    own = own_ref[...]
    gain_out_ref[...] = gain_ref[...]
    qt_ref[...] = across(qkv_ref[0], own).astype(bf16) * bf16(SCALE)
    k[...] = dot(own, qkv_ref[1]).astype(bf16)
    load_values(vt, across(qkv_ref[2], own).astype(bf16), H4)

    def finish(head, peak, mixed):
        peak_ref[head] = peak
        mixed_ref[head] = mixed

    attend(H4, k, qt_ref, vt, s, finish)


def other_kernel(
    other_ref,
    qkv_ref,
    qt_ref,
    peak_ref,
    mixed_ref,
    rows_ref,
    proj_ref,
    weight_ref,
    child_ref,
    place_ref,
    ends_ref,
    out_ref,
    parts_ref,
    k,
    vt,
    s,
    at,
    fine_ref,
    sems,
):
    other = other_ref[...]
    k[...] = dot(other, qkv_ref[1]).astype(bf16)
    load_values(vt, across(qkv_ref[2], other).astype(bf16), H4)
    attend(H4, k, qt_ref, vt, s, divide(at), lambda head: (peak_ref[head], mixed_ref[head]))
    fine = (rows_ref[...].astype(f32) + dot(joined(at), proj_ref[...])).astype(bf16)
    fine_ref[...] = fine
    copies = fetch([(fine_ref, out_ref)], sems)
    pool_own(fine, weight_ref, child_ref, place_ref, ends_ref, parts_ref)
    copies[0].wait()


def coarse_kernel(q_ref, both_ref, proj_ref, out_ref, k, vt, s, qt, at):
    n, width = q_ref.shape
    qt[...] = jnp.transpose(q_ref[...] * bf16(SCALE))
    k[...] = both_ref[:, :width]
    values = both_ref[:, width:]
    load_values(vt, jnp.transpose(values), width // HEAD)
    attend(width // HEAD, k, qt, vt, s, divide(at))
    terms = dot(joined(at), proj_ref[...]).astype(bf16)
    parts = out_ref.shape[0]
    for g in range(parts):
        out_ref[g] = terms[:, g * width : (g + 1) * width]


EDGE = 16


def gelu(values):
    return jax.nn.gelu(values, approximate=True).astype(bf16)


def three_terms(value):
    first = value.astype(bf16).astype(f32)
    second = (value - first).astype(bf16).astype(f32)
    return [first, second, value - first - second]


def run_starts(child_ref, n):
    nx = lax.axis_size("x")
    return child_ref[0:1, :] - lax.axis_index(PTS) * (nx * n)


def own_starts(child_ref, n):
    return run_starts(child_ref, n) - lax.axis_index("x") * n


def ahead(block, k, fill):
    return jnp.concatenate([block[k:], jnp.full((k, block.shape[1]), fill, f32)], axis=0)


def pool_own(fine, weight_ref, child_ref, place_ref, ends_ref, parts_ref):
    n = fine.shape[0]
    groups, total, width = parts_ref.shape
    room = total - EDGE
    start_row = own_starts(child_ref, n)
    last = jnp.max(
        jnp.where(start_row < n, start_row.astype(f32), -1.0), axis=1, keepdims=True
    ).astype(jnp.int32)
    tail = KIDS
    leaving = lax.broadcasted_iota(jnp.int32, (tail, width), 0) + (n - tail) >= last
    edge_row = lax.broadcasted_iota(jnp.int32, (EDGE, width), 0)
    ends = [ends_ref[i] > 0.0 for i in range(ends_ref.shape[0])]
    for g in range(groups):
        best = dot(fine, weight_ref[:, g * width : (g + 1) * width])
        lifted_tail = best[n - tail :]
        for i, end in enumerate(ends):
            best = jnp.where(end, best, jnp.maximum(best, ahead(best, 1 << i, 0.0)))
        parts_ref[g, :room, :] = dot(place_ref[...], gelu(best)).astype(bf16)
        head = jnp.max(jnp.where(leaving, lifted_tail, -jnp.inf), axis=0, keepdims=True)
        edge = jnp.zeros((EDGE, width), f32)
        for at, value in ((0, head), (8, best[0:1])):
            for i, term in enumerate(three_terms(value)):
                edge = jnp.where(edge_row == at + i, term, edge)
        parts_ref[g, room:, :] = edge.astype(bf16)


def count(hits):
    return jnp.sum(jnp.where(hits, 1.0, 0.0), axis=1, keepdims=True).astype(jnp.int32)


def pool_kernel(parts_ref, child_ref, want_ref, out_ref):
    groups, total, width = parts_ref.shape
    room = total - EDGE
    n = out_ref.shape[0]
    start_row = run_starts(child_ref, n)
    spot = lax.broadcasted_iota(jnp.int32, (room, width), 0)

    def edge(g, at):
        block = parts_ref[g, room:, :].astype(f32)
        return block[at : at + 1] + block[at + 1 : at + 2] + block[at + 2 : at + 3]

    parts = []
    for g in range(groups):
        part = parts_ref[g, :room, :]
        if g + 1 < groups:
            whole = gelu(jnp.maximum(edge(g, 0), edge(g + 1, 8))).astype(f32)
            final = count(start_row < (g + 1) * n) - count(start_row < g * n) - 1
            final = jnp.where(count(start_row == (g + 1) * n) > 0, -1, final)
            part = jnp.where(spot == final, whole, part.astype(f32)).astype(bf16)
        parts.append(part)
    out_ref[...] = dot(want_ref[...], jnp.concatenate(parts, axis=0)).astype(bf16)


def spread_kernel(rows_ref, out_ref):
    nz, per_z, width = rows_ref.shape
    parts, copies, part, _ = out_ref.shape
    n = nz * per_z
    rank = per_z // parts
    at = lax.broadcasted_iota(jnp.int32, (n, 1), 0)
    pts = at // part
    source = at % part // rank * per_z + (pts % 2 * (parts // 2) + pts // 2) * rank + at % rank
    moved = dot(one_hot(source, n), rows_ref[...].reshape(n, width)).astype(bf16)
    for i in range(parts):
        for x in range(copies):
            out_ref[i, x] = moved[i * part : (i + 1) * part]


def norm5_kernel(pick_ref, parts_ref, gain_ref, qkv_ref, q_ref, kv_ref, cols_ref):
    n = pick_ref.shape[0]
    groups, width = parts_ref.shape[1], parts_ref.shape[3]
    parts = [parts_ref[:, g].reshape(n, width) for g in range(groups)]
    own = parts_ref[:, pl.ds(lax.axis_index("x"), 1)].reshape(n, width)
    picked = dot(pick_ref[...], jnp.concatenate(parts + [own], axis=1)).astype(bf16)
    rows = picked[:, : groups * width]
    cols_ref[...] = picked[:, groups * width :]
    normed = layer_norm(rows, gain_ref[...])
    q_ref[...] = dot(normed, qkv_ref[0]).astype(bf16)
    kv_ref[:, :width] = dot(normed, qkv_ref[1]).astype(bf16)
    kv_ref[:, width:] = dot(normed, qkv_ref[2]).astype(bf16)


def sum_kernel(cols_ref, parts_ref, out_ref):
    total = cols_ref[...].astype(f32)
    summed = parts_ref[0].astype(f32)
    for g in range(1, parts_ref.shape[0]):
        summed = summed + parts_ref[g].astype(f32)
    out_ref[...] = (total + summed).astype(bf16)


def shape(dims, dtype=bf16):
    return jax.ShapeDtypeStruct(dims, dtype)


def exchange(block, axes):
    return lax.all_to_all(block, axes, split_axis=0, concat_axis=0, tiled=True)


VMEM = pl.BlockSpec(memory_space=pltpu.VMEM)
HBM = pl.BlockSpec(memory_space=pltpu.HBM)
DMA = pltpu.SemaphoreType.DMA


def kernel(body, name, out_shape, scratch=(), flops=0, **extra):
    extra["cost_estimate"] = pl.CostEstimate(
        flops=flops or 1 << 28, bytes_accessed=0, transcendentals=0
    )
    return pl.pallas_call(
        body,
        out_shape=out_shape,
        scratch_shapes=list(scratch),
        compiler_params=pltpu.CompilerParams(vmem_limit_bytes=48 << 20),
        name=name,
        **extra,
    )


def local(
    feats4, order4, gain4, qkv4, proj4, pool_weight, child5, mask5, order5, gain5, qkv5, proj5
):
    n = feats4.shape[0]
    nz = lax.axis_size("z")
    planes = lax.axis_size("y") * lax.axis_size("c") * lax.axis_size("x")
    nx = lax.axis_size("x")

    feats4_pair = lax.all_gather(feats4, "c", axis=0, tiled=True)
    wanted, owner4, slot5 = kernel(
        functools.partial(request_kernel, planes),
        "request",
        [shape((nz, 4, planes // 2), jnp.int32), shape((1, n), jnp.int32), shape((1, n), jnp.int32)],
    )(jnp.stack([order4, order5]))
    by_z = exchange(wanted, ("z",)).transpose(2, 1, 0)
    asked = exchange(by_z.reshape(planes // 2, 4 * nz), ("y", "x"))
    asked_both = lax.all_gather(asked, "c", axis=0, tiled=True)

    chips = n // 2
    outgoing = kernel(pick_kernel, "pick4", shape((chips, 2 * C4)))(asked, feats4_pair)
    arrived = exchange(outgoing.reshape(chips, 4, C4 // 2), CHIPS).reshape(chips, 2 * C4)
    child_rows = child5.T
    width = C5 // nx
    square = shape((n, n))
    room = n - (nx - 1) * (n // KIDS)
    room += -room % EDGE + EDGE
    pick4, pick5, want5, place, ends, gain4 = kernel(
        prepare_kernel,
        "prepare",
        [
            square,
            square,
            shape((n, nx * room)),
            shape((room, n)),
            shape((3, n, width), f32),
            shape((1, C4), f32),
        ],
    )(owner4, slot5, asked_both, child_rows, gain4.reshape(1, C4))
    curve_rows, normed4 = kernel(norm4_kernel, "norm4", [shape((n, C4)), shape((n, C4))])(
        pick4, arrived, gain4
    )
    other4 = lax.ppermute(normed4, "x", [(i, i ^ 1) for i in range(nx)])
    half = 4 * n * n * C4 * H4
    qt4, peak4, mixed4, gain5 = kernel(
        own_kernel,
        "attend4_own",
        [
            shape((C4, n)),
            shape((H4, 1, n), f32),
            shape((H4, 2 * HEAD, n), f32),
            shape((1, C5), f32),
        ],
        attend_scratch(H4, n, n),
        flops=half,
    )(normed4, qkv4, gain5.reshape(1, C5))
    fine_out, parts4 = kernel(
        other_kernel,
        "attend4_other",
        [shape((n, C4)), shape((nx, room + EDGE, width))],
        attend_scratch(H4, n, n)
        + [pltpu.VMEM((H4, HEAD, n), bf16), pltpu.VMEM((n, C4), bf16), DMA((1,))],
        flops=half,
        out_specs=[pl.BlockSpec(memory_space=pl.ANY), VMEM],
    )(other4, qkv4, qt4, peak4, mixed4, curve_rows, proj4, pool_weight, child_rows, place, ends)

    pooled = kernel(pool_kernel, "pool", shape((n, width)))(
        exchange(parts4, "x"), child_rows, want5
    )
    by_z = exchange(pooled.reshape(nz, n // nz, width), ("z",))
    copies = kernel(
        spread_kernel, "spread", shape((planes // nx, nx, n * nx // planes, width))
    )(by_z)
    parts5 = exchange(copies.reshape(planes, n * nx // planes, width), PLANE)
    parts5 = parts5.reshape(copies.shape)
    query5, kv5, own_columns = kernel(
        norm5_kernel,
        "norm5",
        [shape((n, width)), shape((n, 2 * width)), shape((n, width))],
    )(pick5, parts5, gain5, qkv5)
    both5 = lax.all_gather(kv5, "c", axis=0, tiled=True)
    terms = kernel(
        coarse_kernel,
        "attend5",
        shape((nx, n, width)),
        attend_scratch(width // HEAD, n, 2 * n)
        + [pltpu.VMEM((width, n), bf16), pltpu.VMEM((width // HEAD, HEAD, n), bf16)],
    )(query5, both5, proj5)
    coarse_out = kernel(sum_kernel, "add5", shape((n, width)))(own_columns, exchange(terms, "x"))
    return (fine_out, coarse_out)


def solution(mesh):
    pts, grp = mesh.devices.shape
    inner = Mesh(mesh.devices.reshape(pts // 8, 4, 2, grp), ALL)
    in_specs = (
        P(ALL, None),
        P(ALL),
        P(),
        P(),
        P(),
        P(),
        P(PTS, None),
        P(PTS, None),
        P(PTS),
        P(),
        P(None, None, "x"),
        P("x", None),
    )
    out_specs = (P(ALL, None), P(PTS, "x"))
    return jax.shard_map(local, mesh=inner, in_specs=in_specs, out_specs=out_specs, check_vma=False)
```

time: 170 us -> 159 us (0.935)
  blocking collectives: 136 us -> 95.7 us
  starting transfers between devices: 2.37 us -> 20.4 us
  waiting for transfers between devices: 1.28 us -> 13.5 us
  local copies, waits for them, and re-layouts: 4.21 us -> 2.5 us
    all_to_all x7 -> x5, blocking collectives: 134 us -> 84.8 us  [exchange(): return lax.all_to_all(block, axes, split_axis=0, concat_axis=0, tiled=True)]
    all_to_all x0 -> x2, starting transfers between devices: none -> 17 us  [exchange(): return lax.all_to_all(block, axes, split_axis=0, concat_axis=0, tiled=True)]
    all_to_all x0 -> x2, waiting for transfers between devices: none -> 13.5 us  [exchange(): return lax.all_to_all(block, axes, split_axis=0, concat_axis=0, tiled=True)]
    all_gather x0 -> x2, blocking collectives: none -> 8.5 us  [the longest x1 4.34 us: local(): feats4_pair = lax.all_gather(feats4, 'c', axis=0, tiled=True)]
    unnamed x23 -> x21, local copies, waits for them, and re-layouts: 3.77 us -> 0.96 us
    pallas_call x3 -> x5, Pallas kernels: 9.47 us -> 10.2 us  [the longest x1 7.35 us: local(): kernel(other_kernel, 'attend4_other', [shape((n, C4)), shape((nx, room +...]
  transfers between devices with their start and end apart: 1 -> 3, of which waited for: 1 -> 2; matrix products, arithmetic and copies ran while one was open for 0% -> 0% of each run, Pallas kernels for 3% -> 5%
where the time goes in v3:
time: 159 us
  blocking collectives  95.7 us (60%)
  Pallas kernels  24.9 us (16%)
  starting transfers between devices  20.4 us (13%)
  waiting for transfers between devices  13.5 us (8%)
  local copies, waits for them, and re-layouts  2.5 us (2%)
    all_to_all x5, blocking collectives, exchange(): return lax.all_to_all(block, axes, split_axis=0, concat_axis=0, tiled=True)  84.8 us
    all_to_all x2, starting transfers between devices, exchange(): return lax.all_to_all(block, axes, split_axis=0, concat_axis=0, tiled=True)  17 us
    all_to_all x2, waiting for transfers between devices, exchange(): return lax.all_to_all(block, axes, split_axis=0, concat_axis=0, tiled=True)  13.5 us
    pallas_call x1, Pallas kernels, local(): kernel(other_kernel, 'attend4_other', [shape((n, C4)), shape((nx, room +...  7.35 us
    pallas_call x1, Pallas kernels, local(): kernel(own_kernel, 'attend4_own', [shape((C4, n)), shape((H4, 1, n), f32)...  5.73 us
    pallas_call x1, Pallas kernels, local(): kernel(coarse_kernel, 'attend5', shape((nx, n, width)), attend_scratch(wi...  5.06 us
    all_gather x1, blocking collectives, local(): feats4_pair = lax.all_gather(feats4, 'c', axis=0, tiled=True)  4.34 us
    all_gather x1, blocking collectives, local(): asked_both = lax.all_gather(asked, 'c', axis=0, tiled=True)  4.16 us
  transfers between devices with their start and end apart: 3, of which 2 were waited for; matrix products, arithmetic and copies ran while one was open for 0% of the time, Pallas kernels for 5%

profile of v3, /device:TPU:1, one launch (start us, length us, event | category | flops | bytes accessed | tf_op | source)
XLA Modules:
  0.0 158.5 jit_solution(12390431795535429880)
XLA Ops:
  0.6 0.7 pad_add_fusion.orders_ref
  1.3 1.2 request.1
  2.6 27.0 %all_to_all.41 = s32[16,4,16]{2,1,0:T(4,128)S(1)} all-to-all(s32[16,4,16]{2,1,0:T(4,128)S(1)} %get-tuple-element.24), channel_id=1, replica_groups=mesh['z'=16,'y'=4,'c'=2,'x'=4] {'z'}, dimensions={0} | all-to-all | bytes 8192 | tf_op jit(solution)/shard_map/all_to_all | solution.py:443
  29.6 0.1 copy.15
  29.7 0.7 all_to_all.26
  30.4 6.9 %all-to-all-start.1 = ((s32[16,1,64]{2,1,0:T(1,128)}), s32[16,1,64]{2,1,0:T(1,128)S(1)}, u32[]{:S(2)}, u32[]{:S(2)}) async-start(s32[16,1,64]{2,1,0:T(1,128)} %bitcast.3), calls=%async_computation.1 | async-start | bytes 16384 | tf_op jit(solution)/shard_map/all_to_all | solution.py:443
  37.3 4.3 %all_gather.10.table_ref = bf16[1024,256]{1,0:T(8,128)(2,1)S(1)} all-gather(bf16[512,256]{1,0:T(8,128)(2,1)} %param.12), channel_id=1, replica_groups=mesh['z'=16,'y'=4,'c'=2,'x'=4] {'c'}, dimensions={0}, use_global_device_ids=true | all-gather | bytes 786432 | tf_op jit(solution)/shard_map/all_gather | solution.py:473
  41.6 2.0 %all-to-all-done.1 = s32[16,1,64]{2,1,0:T(1,128)S(1)} async-done(((s32[16,1,64]{2,1,0:T(1,128)}), s32[16,1,64]{2,1,0:T(1,128)S(1)}, u32[]{:S(2)}, u32[]{:S(2)}) %all-to-all-start.1) | async-done | bytes 4128 | tf_op jit(solution)/shard_map/all_to_all | solution.py:443
  43.6 0.4 pick4.1
  44.0 0.8 reshape.30
  44.7 10.1 %all-to-all-start.2 = ((bf16[256,4,128]{2,1,0:T(4,128)(2,1)}), bf16[256,4,128]{2,1,0:T(4,128)(2,1)S(1)}, u32[]{:S(2)}, u32[]{:S(2)}) async-start(bf16[256,4,128]{2,1,0:T(4,128)(2,1)} %reshape.30), calls=%async_computation.2 | async-start | bytes 524288 | tf_op jit(solution)/shard_map/all_to_all | solution.py:443
  54.9 4.2 %all-gather = s32[32,1,64]{2,0,1:T(8,128)S(1)} all-gather(s32[16,1,64]{2,0,1:T(8,128)S(1)} %bitcast.22), channel_id=2, replica_groups=mesh['z'=16,'y'=4,'c'=2,'x'=4] {'c'}, dimensions={0}, use_global_device_ids=true | all-gather | bytes 12288 | tf_op jit(solution)/shard_map/all_gather | solution.py:481
  59.0 1.7 %prepare.1 = (bf16[512,512]{1,0:T(8,128)(2,1)S(1)}, bf16[512,512]{1,0:T(8,128)(2,1)S(1)}, bf16[512,1344]{1,0:T(8,128)(2,1)S(1)}, bf16[336,512]{1,0:T(8,128)(2,1)...) custom-call(s32[1,512]{1,0:T(1,128)S(1)} %get-tuple-element.22.owner_ref, ...), custom_call_target="tpu_custom_call" | custom-call | flops 268435456 | tf_op jit(solution)/shard_map/prepare/pallas_call | solution.py:491
  60.8 0.9 copy-done.8
  61.6 11.5 %all-to-all-done.2 = bf16[256,4,128]{2,1,0:T(4,128)(2,1)S(1)} async-done(((bf16[256,4,128]{2,1,0:T(4,128)(2,1)}), bf16[256,4,128]{2,1,0:T(4,128)(2,1)S(1)}, u32[]{:S(2)}, u32[]{:S(2)}) %all-to-all-start.2) | async-done | bytes 262176 | tf_op jit(solution)/shard_map/all_to_all | solution.py:443
  73.2 0.5 norm4.1
  73.6 3.4 %collective-permute-start = (bf16[512,256]{1,0:T(8,128)(2,1)S(1)}, bf16[512,256]{1,0:T(8,128)(2,1)S(1)}, u32[]{:S(2)}, u32[]{:S(2)}) collective-permute-start(bf16[512,256]{1,0:T(8,128)(2,1)S(1)} %get-tuple-element.27.own_ref), channel_id=1, source_target_pairs={{0,1},{1,0},{2,3},{3,2},{4,5},{5,4},{6,7},{7,6},{8,9},{9,8},{10,11... | collective-permute-start | bytes 786440 | tf_op jit(solution)/shard_map/ppermute | solution.py:506
  77.1 0.0 copy-start.4
  77.1 0.0 copy-start.5
  77.1 5.7 %attend4_own.1 = (bf16[256,512]{1,0:T(8,128)(2,1)S(1)}, f32[16,1,512]{2,1,0:T(1,128)S(1)}, f32[16,32,512]{2,1,0:T(8,128)S(1)}, f32[1,512]{1,0:T(1,128)S(1)}) custom-call(bf16[512,256]{1,0:T(8,128)(2,1)S(1)} %get-tuple-element.27.own_ref, bf16[3,256,256]{2,1,0:T(8,128)(2,1)S(1)} %copy-done.3, f32[1,512]{1,0:T(1,128)S(1)} %bitcast.27), custom_call_target="tpu_custom_call" | custom-call | flops 4294967296 | tf_op jit(solution)/shard_map/attend4_own/pallas_call | solution.py:508
  82.9 7.4 %attend4_other.1 = (bf16[512,256]{1,0:T(8,128)(2,1)}, bf16[4,352,128]{2,1,0:T(8,128)(2,1)S(1)}) custom-call(bf16[512,256]{1,0:T(8,128)(2,1)S(1)} %collective-permute-done.other_ref, bf16[3,256,256]{2,1,0:T(8,128)(2,1)S(1)} %copy-done.3, bf16[256,512]{1,0:T(8,128)(2,1)S(1)} %get-tuple-element.28.qt_ref, f32[16,1,512]{2,1,0:T(1,128)S(1)} %get-tuple-element.29.peak_ref, ...), custom_call_target="tpu_custom_call" | custom-call | flops 4294967296 | tf_op jit(solution)/shard_map/attend4_other/pallas_call | solution.py:520
  90.3 9.0 %all_to_all.42.parts_ref = bf16[4,352,128]{2,1,0:T(8,128)(2,1)S(1)} all-to-all(bf16[4,352,128]{2,1,0:T(8,128)(2,1)S(1)} %get-tuple-element.36), channel_id=1, replica_groups=mesh['z'=16,'y'=4,'c'=2,'x'=4] {'x'}, dimensions={0} | all-to-all | bytes 720896 | tf_op jit(solution)/shard_map/all_to_all | solution.py:443
  99.3 0.7 pool.1
  100.0 0.0 copy-start
  100.0 16.6 %all_to_all.43.rows_ref = bf16[16,32,128]{2,1,0:T(8,128)(2,1)S(1)} all-to-all(bf16[16,32,128]{2,1,0:T(8,128)(2,1)S(1)} %bitcast.19), channel_id=1, replica_groups=mesh['z'=16,'y'=4,'c'=2,'x'=4] {'z'}, dimensions={0} | all-to-all | bytes 262144 | tf_op jit(solution)/shard_map/all_to_all | solution.py:443
  116.5 0.3 spread.1
  116.9 20.6 %all_to_all.44 = bf16[32,64,128]{2,1,0:T(8,128)(2,1)S(1)} all-to-all(bf16[32,64,128]{2,1,0:T(8,128)(2,1)S(1)} %bitcast.18), channel_id=1, replica_groups=mesh['z'=16,'y'=4,'c'=2,'x'=4] {'y','c','x'}, dimensions={0} | all-to-all | bytes 1048576 | tf_op jit(solution)/shard_map/all_to_all | solution.py:443
  137.5 1.3 norm5.1
  138.8 2.4 %all_gather.11.both_ref = bf16[1024,256]{1,0:T(8,128)(2,1)S(1)} all-gather(bf16[512,256]{1,0:T(8,128)(2,1)S(1)} %get-tuple-element.41), channel_id=1, replica_groups=mesh['z'=16,'y'=4,'c'=2,'x'=4] {'c'}, dimensions={0}, use_global_device_ids=true | all-gather | bytes 786432 | tf_op jit(solution)/shard_map/all_gather | solution.py:544
  141.1 5.1 %attend5.1 = bf16[4,512,128]{2,1,0:T(8,128)(2,1)S(1)} custom-call(bf16[512,128]{1,0:T(8,128)(2,1)S(1)} %get-tuple-element.40.q_ref, bf16[1024,256]{1,0:T(8,128)(2,1)S(1)} %all_gather.11.both_ref, bf16[128,512]{1,0:T(8,128)(2,1)S(1)} %copy-done.1), custom_call_target="tpu_custom_call" | custom-call | flops 268435456 | tf_op jit(solution)/shard_map/attend5/pallas_call | solution.py:545
  146.2 11.6 %all_to_all.45.parts_ref = bf16[4,512,128]{2,1,0:T(8,128)(2,1)S(1)} all-to-all(bf16[4,512,128]{2,1,0:T(8,128)(2,1)S(1)} %attend5.1), channel_id=1, replica_groups=mesh['z'=16,'y'=4,'c'=2,'x'=4] {'x'}, dimensions={0} | all-to-all | bytes 1048576 | tf_op jit(solution)/shard_map/all_to_all | solution.py:443
  157.8 0.7 add5.1
  (18 shorter events, 0.1 us)
Async XLA Ops:
  30.4 28.7 %copy-start.2 = (s32[512,8]{0,1:T(8,128)S(1)}, s32[512,8]{0,1:T(8,128)}, u32[]{:S(2)}) copy-start(s32[512,8]{0,1:T(8,128)} %param.18) | copy-start | bytes 49156
  30.4 28.7 %copy-start.7 = (f32[256]{0:T(256)S(1)}, f32[256]{0:T(256)}, u32[]{:S(2)}) copy-start(f32[256]{0:T(256)} %param.14) | copy-start | bytes 3076
  30.4 13.2 %all-to-all-start.1 = ((s32[16,1,64]{2,1,0:T(1,128)}), s32[16,1,64]{2,1,0:T(1,128)S(1)}, u32[]{:S(2)}, u32[]{:S(2)}) async-start(s32[16,1,64]{2,1,0:T(1,128)} %bitcast.3), calls=%async_computation.1 | async-start | bytes 16384 | tf_op jit(solution)/shard_map/all_to_all | solution.py:443
  44.7 32.4 %copy-start.3 = (bf16[3,256,256]{2,1,0:T(8,128)(2,1)S(1)}, bf16[3,256,256]{2,1,0:T(8,128)(2,1)}, u32[]{:S(2)}) copy-start(bf16[3,256,256]{2,1,0:T(8,128)(2,1)} %qkv_ref.4) | copy-start | bytes 1179652
  44.7 32.4 %copy-start.6 = (f32[512]{0:T(512)S(1)}, f32[512]{0:T(512)}, u32[]{:S(2)}) copy-start(f32[512]{0:T(512)} %param.20) | copy-start | bytes 6148
  44.7 28.4 %all-to-all-start.2 = ((bf16[256,4,128]{2,1,0:T(4,128)(2,1)}), bf16[256,4,128]{2,1,0:T(4,128)(2,1)S(1)}, u32[]{:S(2)}, u32[]{:S(2)}) async-start(bf16[256,4,128]{2,1,0:T(4,128)(2,1)} %reshape.30), calls=%async_computation.2 | async-start | bytes 524288 | tf_op jit(solution)/shard_map/all_to_all | solution.py:443
  60.7 0.9 copy-start.8
  73.6 9.2 %collective-permute-start = (bf16[512,256]{1,0:T(8,128)(2,1)S(1)}, bf16[512,256]{1,0:T(8,128)(2,1)S(1)}, u32[]{:S(2)}, u32[]{:S(2)}) collective-permute-start(bf16[512,256]{1,0:T(8,128)(2,1)S(1)} %get-tuple-element.27.own_ref), channel_id=1, source_target_pairs={{0,1},{1,0},{2,3},{3,2},{4,5},{5,4},{6,7},{7,6},{8,9},{9,8},{10,11... | collective-permute-start | bytes 786440 | tf_op jit(solution)/shard_map/ppermute | solution.py:506
  77.1 5.8 %copy-start.4 = (bf16[256,512]{1,0:T(8,128)(2,1)S(1)}, bf16[256,512]{1,0:T(8,128)(2,1)}, u32[]{:S(2)}) copy-start(bf16[256,512]{1,0:T(8,128)(2,1)} %weight_ref.1) | copy-start | bytes 786436
  77.1 5.8 %copy-start.5 = (bf16[256,256]{1,0:T(8,128)(2,1)S(1)}, bf16[256,256]{1,0:T(8,128)(2,1)}, u32[]{:S(2)}) copy-start(bf16[256,256]{1,0:T(8,128)(2,1)} %proj_ref.2) | copy-start | bytes 393220
  77.1 5.8 %copy-start.9 = (f32[3,512,128]{2,1,0:T(8,128)S(1)}, f32[3,512,128]{2,1,0:T(8,128)}, u32[]{:S(2)}) copy-start(f32[3,512,128]{2,1,0:T(8,128)} %copy-done.8) | copy-start | bytes 2359300
  100.0 37.5 %copy-start = (bf16[3,512,128]{2,1,0:T(8,128)(2,1)S(1)}, bf16[3,512,128]{2,1,0:T(8,128)(2,1)}, u32[]{:S(2)}) copy-start(bf16[3,512,128]{2,1,0:T(8,128)(2,1)} %qkv_ref.5) | copy-start | bytes 1179652
  116.9 24.3 %copy-start.1 = (bf16[128,512]{1,0:T(8,128)(2,1)S(1)}, bf16[128,512]{1,0:T(8,128)(2,1)}, u32[]{:S(2)}) copy-start(bf16[128,512]{1,0:T(8,128)(2,1)} %proj_ref.3) | copy-start | bytes 393220

commit v4 on v3

--- a/solution.py
+++ b/solution.py
@@ -32,13 +32,6 @@
 
 def column(row):
     return jnp.transpose(jnp.broadcast_to(row, (8, row.shape[1])))[:, :1]
-
-
-def columns(*rows):
-    n = rows[0].shape[1]
-    fill = [jnp.zeros((8 - len(rows), n), jnp.int32)] if len(rows) < 8 else []
-    block = jnp.transpose(jnp.concatenate(list(rows) + fill, axis=0))
-    return [block[:, i : i + 1] for i in range(len(rows))]
 
 
 def one_hot(col, width):
@@ -72,31 +65,30 @@
     owner_ref[...] = u // nx % 2 * (n // 2) + owner4 // planes * half + lane4 % half
     of_pts = owner5 % per_z
     pair5 = of_pts % 2 * ny + of_pts // 2
-    lane4_col, row4_col, owner5_col, pair5_col, row5_col = columns(
-        lane4, o4 % n, owner5, pair5, o5 % n
-    )
 
     lanes = lax.broadcasted_iota(jnp.int32, (n, n), 1)
     rows = lax.broadcasted_iota(jnp.int32, (n, n), 0)
-    earlier = jnp.where((owner5_col == owner5) & (rows < lanes), 1.0, 0.0)
+    earlier = jnp.where((column(owner5) == owner5) & (rows < lanes), 1.0, 0.0)
     rank = jnp.sum(earlier, axis=0, keepdims=True).astype(jnp.int32)
-    slot_ref[...] = ((owner5 % per_z) * nz + owner5 // per_z) * nx + rank
-
-    lane = lax.broadcasted_iota(jnp.int32, (n, planes), 1)
+    slot_ref[...] = (of_pts * nz + owner5 // per_z) * nx + rank
+
+    place = lax.broadcasted_iota(jnp.int32, (planes, n), 0)
     zs = lax.broadcasted_iota(jnp.int32, (nz, n), 0)
 
     def table(z_hit, u_hit, row):
         low = jnp.where(u_hit, (row % 256).astype(f32), 0.0)
         high = jnp.where(u_hit, (row // 256).astype(f32), 0.0)
-        both = dot(
+        both = lax.dot_general(
             jnp.where(z_hit, 1.0, 0.0).astype(bf16),
-            jnp.concatenate([low, high], axis=1).astype(bf16),
+            jnp.concatenate([low, high], axis=0).astype(bf16),
+            (((1,), (1,)), ((), ())),
+            preferred_element_type=f32,
         )
         return (both[:, :planes] + 256.0 * both[:, planes:]).astype(jnp.int32)
 
-    want4 = table(zs == owner4 // planes, lane4_col == lane, row4_col)
+    want4 = table(zs == owner4 // planes, place == lane4, o4 % n)
     own_rank = (zs == owner5 // per_z) & (rank == x)
-    want5 = table(own_rank, pair5_col == lane // nx, row5_col)
+    want5 = table(own_rank, place // nx == pair5, o5 % n)
     for c in range(2):
         out_ref[:, c, :] = want4[:, c * half : (c + 1) * half]
         out_ref[:, 2 + c, :] = want5[:, c * half : (c + 1) * half]
@@ -422,9 +414,10 @@
     rows = picked[:, : groups * width]
     cols_ref[...] = picked[:, groups * width :]
     normed = layer_norm(rows, gain_ref[...])
-    q_ref[...] = dot(normed, qkv_ref[0]).astype(bf16)
-    kv_ref[:, :width] = dot(normed, qkv_ref[1]).astype(bf16)
-    kv_ref[:, width:] = dot(normed, qkv_ref[2]).astype(bf16)
+    weights = jnp.concatenate([qkv_ref[i] for i in range(3)], axis=1)
+    projected = dot(normed, weights).astype(bf16)
+    q_ref[...] = projected[:, :width]
+    kv_ref[...] = projected[:, width:]
 
 
 def sum_kernel(cols_ref, parts_ref, out_ref):
@@ -477,6 +470,7 @@
         [shape((nz, 4, planes // 2), jnp.int32), shape((1, n), jnp.int32), shape((1, n), jnp.int32)],
     )(jnp.stack([order4, order5]))
     by_z = exchange(wanted, ("z",)).transpose(2, 1, 0)
+    by_z, feats4_pair = lax.optimization_barrier((by_z, feats4_pair))
     asked = exchange(by_z.reshape(planes // 2, 4 * nz), ("y", "x"))
     asked_both = lax.all_gather(asked, "c", axis=0, tiled=True)
 

time: 159 us -> 157 us (0.987)
  blocking collectives: 95.7 us -> 81.7 us
  starting transfers between devices: 20.4 us -> 28.2 us
  waiting for transfers between devices: 13.5 us -> 18.8 us
    all_to_all x5, blocking collectives: 84.8 us -> 71.4 us  [exchange(): return lax.all_to_all(block, axes, split_axis=0, concat_axis=0, tiled=True)]
    all_to_all x2, starting transfers between devices: 17 us -> 25 us  [exchange(): return lax.all_to_all(block, axes, split_axis=0, concat_axis=0, tiled=True)]
    all_to_all x2, waiting for transfers between devices: 13.5 us -> 18.7 us  [exchange(): return lax.all_to_all(block, axes, split_axis=0, concat_axis=0, tiled=True)]
where the time goes in v4:
time: 157 us
  blocking collectives  81.7 us (52%)
  starting transfers between devices  28.2 us (18%)
  Pallas kernels  24.8 us (16%)
  waiting for transfers between devices  18.8 us (12%)
  local copies, waits for them, and re-layouts  1.9 us (1%)
    all_to_all x5, blocking collectives, exchange(): return lax.all_to_all(block, axes, split_axis=0, concat_axis=0, tiled=True)  71.4 us
    all_to_all x2, starting transfers between devices, exchange(): return lax.all_to_all(block, axes, split_axis=0, concat_axis=0, tiled=True)  25 us
    all_to_all x2, waiting for transfers between devices, exchange(): return lax.all_to_all(block, axes, split_axis=0, concat_axis=0, tiled=True)  18.7 us
    pallas_call x1, Pallas kernels, local(): kernel(other_kernel, 'attend4_other', [shape((n, C4)), shape((nx, room +...  7.35 us
    pallas_call x1, Pallas kernels, local(): kernel(own_kernel, 'attend4_own', [shape((C4, n)), shape((H4, 1, n), f32)...  5.73 us
    pallas_call x1, Pallas kernels, local(): kernel(coarse_kernel, 'attend5', shape((nx, n, width)), attend_scratch(wi...  5.07 us
    all_gather x1, blocking collectives, local(): asked_both = lax.all_gather(asked, 'c', axis=0, tiled=True)  4.97 us
  transfers between devices with their start and end apart: 3, of which 2 were waited for; matrix products, arithmetic and copies ran while one was open for 0% of the time, Pallas kernels for 5%

profile of v4, /device:TPU:1, one launch (start us, length us, event | category | flops | bytes accessed | tf_op | source)
XLA Modules:
  0.0 156.9 jit_solution(9417771446610247680)
XLA Ops:
  0.6 0.7 pad_add_fusion.orders_ref
  1.3 1.3 request.1
  2.6 15.7 %all-to-all-start = ((s32[16,4,16]{2,1,0:T(4,128)}), s32[16,4,16]{2,1,0:T(4,128)S(1)}, u32[]{:S(2)}, u32[]{:S(2)}) async-start(s32[16,4,16]{2,1,0:T(4,128)} %get-tuple-element.26), calls=%async_computation | async-start | bytes 65536 | tf_op jit(solution)/shard_map/all_to_all | solution.py:436
  18.3 0.0 copy-start.2
  18.4 3.0 %all_gather.9.table_ref = bf16[1024,256]{1,0:T(8,128)(2,1)S(1)} all-gather(bf16[512,256]{1,0:T(8,128)(2,1)} %param.12), channel_id=1, replica_groups=mesh['z'=16,'y'=4,'c'=2,'x'=4] {'c'}, dimensions={0}, use_global_device_ids=true | all-gather | bytes 786432 | tf_op jit(solution)/shard_map/all_gather | solution.py:466
  21.3 8.5 %all-to-all-done = s32[16,4,16]{2,1,0:T(4,128)S(1)} async-done(((s32[16,4,16]{2,1,0:T(4,128)}), s32[16,4,16]{2,1,0:T(4,128)S(1)}, u32[]{:S(2)}, u32[]{:S(2)}) %all-to-all-start) | async-done | bytes 4128 | tf_op jit(solution)/shard_map/all_to_all | solution.py:436
  29.8 0.1 copy.15
  29.9 0.1 all_to_all.26
  30.0 13.0 %all_to_all.41 = s32[16,1,64]{2,1,0:T(1,128)S(1)} all-to-all(s32[16,1,64]{2,1,0:T(1,128)S(1)} %bitcast.31), channel_id=1, replica_groups=mesh['z'=16,'y'=4,'c'=2,'x'=4] {'y','x'}, dimensions={0} | all-to-all | bytes 8192 | tf_op jit(solution)/shard_map/all_to_all | solution.py:436
  42.9 0.4 pick4.1
  43.3 0.8 reshape.30
  44.1 9.3 %all-to-all-start.2 = ((bf16[256,4,128]{2,1,0:T(4,128)(2,1)}), bf16[256,4,128]{2,1,0:T(4,128)(2,1)S(1)}, u32[]{:S(2)}, u32[]{:S(2)}) async-start(bf16[256,4,128]{2,1,0:T(4,128)(2,1)} %reshape.30), calls=%async_computation.2 | async-start | bytes 524288 | tf_op jit(solution)/shard_map/all_to_all | solution.py:436
  53.4 5.0 %all-gather = s32[32,1,64]{2,0,1:T(8,128)S(1)} all-gather(s32[16,1,64]{2,0,1:T(8,128)S(1)} %bitcast.22), channel_id=2, replica_groups=mesh['z'=16,'y'=4,'c'=2,'x'=4] {'c'}, dimensions={0}, use_global_device_ids=true | all-gather | bytes 12288 | tf_op jit(solution)/shard_map/all_gather | solution.py:475
  58.4 1.7 %prepare.1 = (bf16[512,512]{1,0:T(8,128)(2,1)S(1)}, bf16[512,512]{1,0:T(8,128)(2,1)S(1)}, bf16[512,1344]{1,0:T(8,128)(2,1)S(1)}, bf16[336,512]{1,0:T(8,128)(2,1)...) custom-call(s32[1,512]{1,0:T(1,128)S(1)} %get-tuple-element.24.owner_ref, ...), custom_call_target="tpu_custom_call" | custom-call | flops 268435456 | tf_op jit(solution)/shard_map/prepare/pallas_call | solution.py:485
  60.1 0.9 copy-done.8
  61.0 10.3 %all-to-all-done.2 = bf16[256,4,128]{2,1,0:T(4,128)(2,1)S(1)} async-done(((bf16[256,4,128]{2,1,0:T(4,128)(2,1)}), bf16[256,4,128]{2,1,0:T(4,128)(2,1)S(1)}, u32[]{:S(2)}, u32[]{:S(2)}) %all-to-all-start.2) | async-done | bytes 262176 | tf_op jit(solution)/shard_map/all_to_all | solution.py:436
  71.3 0.5 norm4.1
  71.8 3.1 %collective-permute-start = (bf16[512,256]{1,0:T(8,128)(2,1)S(1)}, bf16[512,256]{1,0:T(8,128)(2,1)S(1)}, u32[]{:S(2)}, u32[]{:S(2)}) collective-permute-start(bf16[512,256]{1,0:T(8,128)(2,1)S(1)} %get-tuple-element.31.own_ref), channel_id=1, source_target_pairs={{0,1},{1,0},{2,3},{3,2},{4,5},{5,4},{6,7},{7,6},{8,9},{9,8},{10,11... | collective-permute-start | bytes 786440 | tf_op jit(solution)/shard_map/ppermute | solution.py:500
  74.9 0.0 copy-start.5
  75.0 5.7 %attend4_own.1 = (bf16[256,512]{1,0:T(8,128)(2,1)S(1)}, f32[16,1,512]{2,1,0:T(1,128)S(1)}, f32[16,32,512]{2,1,0:T(8,128)S(1)}, f32[1,512]{1,0:T(1,128)S(1)}) custom-call(bf16[512,256]{1,0:T(8,128)(2,1)S(1)} %get-tuple-element.31.own_ref, bf16[3,256,256]{2,1,0:T(8,128)(2,1)S(1)} %copy-done.3, f32[1,512]{1,0:T(1,128)S(1)} %bitcast.27), custom_call_target="tpu_custom_call" | custom-call | flops 4294967296 | tf_op jit(solution)/shard_map/attend4_own/pallas_call | solution.py:502
  80.7 7.4 %attend4_other.1 = (bf16[512,256]{1,0:T(8,128)(2,1)}, bf16[4,352,128]{2,1,0:T(8,128)(2,1)S(1)}) custom-call(bf16[512,256]{1,0:T(8,128)(2,1)S(1)} %collective-permute-done.other_ref, bf16[3,256,256]{2,1,0:T(8,128)(2,1)S(1)} %copy-done.3, bf16[256,512]{1,0:T(8,128)(2,1)S(1)} %get-tuple-element.32.qt_ref, f32[16,1,512]{2,1,0:T(1,128)S(1)} %get-tuple-element.33.peak_ref, ...), custom_call_target="tpu_custom_call" | custom-call | flops 4294967296 | tf_op jit(solution)/shard_map/attend4_other/pallas_call | solution.py:514
  88.1 9.2 %all_to_all.42.parts_ref = bf16[4,352,128]{2,1,0:T(8,128)(2,1)S(1)} all-to-all(bf16[4,352,128]{2,1,0:T(8,128)(2,1)S(1)} %get-tuple-element.40), channel_id=1, replica_groups=mesh['z'=16,'y'=4,'c'=2,'x'=4] {'x'}, dimensions={0} | all-to-all | bytes 720896 | tf_op jit(solution)/shard_map/all_to_all | solution.py:436
  97.3 0.7 pool.1
  98.0 0.0 copy-start
  98.0 16.3 %all_to_all.43.rows_ref = bf16[16,32,128]{2,1,0:T(8,128)(2,1)S(1)} all-to-all(bf16[16,32,128]{2,1,0:T(8,128)(2,1)S(1)} %bitcast.19), channel_id=1, replica_groups=mesh['z'=16,'y'=4,'c'=2,'x'=4] {'z'}, dimensions={0} | all-to-all | bytes 262144 | tf_op jit(solution)/shard_map/all_to_all | solution.py:436
  114.3 0.3 spread.1
  114.6 21.3 %all_to_all.44 = bf16[32,64,128]{2,1,0:T(8,128)(2,1)S(1)} all-to-all(bf16[32,64,128]{2,1,0:T(8,128)(2,1)S(1)} %bitcast.18), channel_id=1, replica_groups=mesh['z'=16,'y'=4,'c'=2,'x'=4] {'y','c','x'}, dimensions={0} | all-to-all | bytes 1048576 | tf_op jit(solution)/shard_map/all_to_all | solution.py:436
  135.9 1.2 norm5.1
  137.1 2.4 %all_gather.11.both_ref = bf16[1024,256]{1,0:T(8,128)(2,1)S(1)} all-gather(bf16[512,256]{1,0:T(8,128)(2,1)S(1)} %get-tuple-element.45), channel_id=1, replica_groups=mesh['z'=16,'y'=4,'c'=2,'x'=4] {'c'}, dimensions={0}, use_global_device_ids=true | all-gather | bytes 786432 | tf_op jit(solution)/shard_map/all_gather | solution.py:538
  139.5 5.1 %attend5.1 = bf16[4,512,128]{2,1,0:T(8,128)(2,1)S(1)} custom-call(bf16[512,128]{1,0:T(8,128)(2,1)S(1)} %get-tuple-element.44.q_ref, bf16[1024,256]{1,0:T(8,128)(2,1)S(1)} %all_gather.11.both_ref, bf16[128,512]{1,0:T(8,128)(2,1)S(1)} %copy-done.1), custom_call_target="tpu_custom_call" | custom-call | flops 268435456 | tf_op jit(solution)/shard_map/attend5/pallas_call | solution.py:539
  144.5 11.6 %all_to_all.45.parts_ref = bf16[4,512,128]{2,1,0:T(8,128)(2,1)S(1)} all-to-all(bf16[4,512,128]{2,1,0:T(8,128)(2,1)S(1)} %attend5.1), channel_id=1, replica_groups=mesh['z'=16,'y'=4,'c'=2,'x'=4] {'x'}, dimensions={0} | all-to-all | bytes 1048576 | tf_op jit(solution)/shard_map/all_to_all | solution.py:436
  156.1 0.7 add5.1
  (18 shorter events, 0.1 us)
Async XLA Ops:
  2.6 27.2 %all-to-all-start = ((s32[16,4,16]{2,1,0:T(4,128)}), s32[16,4,16]{2,1,0:T(4,128)S(1)}, u32[]{:S(2)}, u32[]{:S(2)}) async-start(s32[16,4,16]{2,1,0:T(4,128)} %get-tuple-element.26), calls=%async_computation | async-start | bytes 65536 | tf_op jit(solution)/shard_map/all_to_all | solution.py:436
  18.3 40.0 %copy-start.2 = (s32[512,8]{0,1:T(8,128)S(1)}, s32[512,8]{0,1:T(8,128)}, u32[]{:S(2)}) copy-start(s32[512,8]{0,1:T(8,128)} %param.18) | copy-start | bytes 49156
  18.4 40.0 %copy-start.7 = (f32[256]{0:T(256)S(1)}, f32[256]{0:T(256)}, u32[]{:S(2)}) copy-start(f32[256]{0:T(256)} %param.14) | copy-start | bytes 3076
  44.1 30.8 %copy-start.3 = (bf16[3,256,256]{2,1,0:T(8,128)(2,1)S(1)}, bf16[3,256,256]{2,1,0:T(8,128)(2,1)}, u32[]{:S(2)}) copy-start(bf16[3,256,256]{2,1,0:T(8,128)(2,1)} %qkv_ref.4) | copy-start | bytes 1179652
  44.1 30.8 %copy-start.6 = (f32[512]{0:T(512)S(1)}, f32[512]{0:T(512)}, u32[]{:S(2)}) copy-start(f32[512]{0:T(512)} %param.20) | copy-start | bytes 6148
  44.1 27.2 %all-to-all-start.2 = ((bf16[256,4,128]{2,1,0:T(4,128)(2,1)}), bf16[256,4,128]{2,1,0:T(4,128)(2,1)S(1)}, u32[]{:S(2)}, u32[]{:S(2)}) async-start(bf16[256,4,128]{2,1,0:T(4,128)(2,1)} %reshape.30), calls=%async_computation.2 | async-start | bytes 524288 | tf_op jit(solution)/shard_map/all_to_all | solution.py:436
  60.1 0.9 copy-start.8
  71.8 8.9 %collective-permute-start = (bf16[512,256]{1,0:T(8,128)(2,1)S(1)}, bf16[512,256]{1,0:T(8,128)(2,1)S(1)}, u32[]{:S(2)}, u32[]{:S(2)}) collective-permute-start(bf16[512,256]{1,0:T(8,128)(2,1)S(1)} %get-tuple-element.31.own_ref), channel_id=1, source_target_pairs={{0,1},{1,0},{2,3},{3,2},{4,5},{5,4},{6,7},{7,6},{8,9},{9,8},{10,11... | collective-permute-start | bytes 786440 | tf_op jit(solution)/shard_map/ppermute | solution.py:500
  74.9 5.8 %copy-start.4 = (bf16[256,512]{1,0:T(8,128)(2,1)S(1)}, bf16[256,512]{1,0:T(8,128)(2,1)}, u32[]{:S(2)}) copy-start(bf16[256,512]{1,0:T(8,128)(2,1)} %weight_ref.1) | copy-start | bytes 786436
  74.9 5.8 %copy-start.5 = (bf16[256,256]{1,0:T(8,128)(2,1)S(1)}, bf16[256,256]{1,0:T(8,128)(2,1)}, u32[]{:S(2)}) copy-start(bf16[256,256]{1,0:T(8,128)(2,1)} %proj_ref.2) | copy-start | bytes 393220
  74.9 5.8 %copy-start.9 = (f32[3,512,128]{2,1,0:T(8,128)S(1)}, f32[3,512,128]{2,1,0:T(8,128)}, u32[]{:S(2)}) copy-start(f32[3,512,128]{2,1,0:T(8,128)} %copy-done.8) | copy-start | bytes 2359300
  98.0 38.0 %copy-start = (bf16[3,512,128]{2,1,0:T(8,128)(2,1)S(1)}, bf16[3,512,128]{2,1,0:T(8,128)(2,1)}, u32[]{:S(2)}) copy-start(bf16[3,512,128]{2,1,0:T(8,128)(2,1)} %qkv_ref.5) | copy-start | bytes 1179652
  114.6 24.9 %copy-start.1 = (bf16[128,512]{1,0:T(8,128)(2,1)S(1)}, bf16[128,512]{1,0:T(8,128)(2,1)}, u32[]{:S(2)}) copy-start(bf16[128,512]{1,0:T(8,128)(2,1)} %proj_ref.3) | copy-start | bytes 393220

commit v5 on v4

--- a/solution.py
+++ b/solution.py
@@ -167,15 +167,21 @@
     normed_ref[...] = layer_norm(rows, gain_ref[...])
 
 
+TOGETHER = 2
+SUMS = (TOGETHER + 1) * HEAD
+
+
 def attend(heads, k_ref, qt_ref, vt_ref, s_ref, finish, before=None, chunk=512):
-    width = heads * HEAD
-    queries = qt_ref.shape[1]
+    steps = heads // TOGETHER
+    queries = s_ref.shape[2]
     keys = k_ref.shape[0]
-    row_head = lax.broadcasted_iota(jnp.int32, (width, queries), 0) // HEAD
-
-    def of_head(head):
+    row_head = lax.broadcasted_iota(jnp.int32, qt_ref.shape, 0) // HEAD
+
+    def of_step(step):
         q = qt_ref[...]
-        return jnp.where(row_head == head, q, jnp.zeros_like(q))
+        none = jnp.zeros_like(q)
+        each = [jnp.where(row_head == step * TOGETHER + i, q, none) for i in range(TOGETHER)]
+        return jnp.concatenate(each, axis=1)
 
     def score(q_head, slot, c, top):
         s = dot(k_ref[c * chunk : (c + 1) * chunk, :], q_head)
@@ -187,13 +193,13 @@
 
     def step(head, slot, peak, more):
         if before is None:
-            mixed = jnp.zeros((2 * HEAD, queries), f32)
+            mixed = jnp.zeros((SUMS, queries), f32)
         else:
             earlier, mixed = before(head)
             peak = jnp.maximum(peak, earlier)
             mixed = mixed * jnp.exp(earlier - peak)
         top = low()
-        q_next = of_head(head + 1) if more else None
+        q_next = of_step(head + 1) if more else None
         for c in range(keys // chunk):
             if more:
                 top = score(q_next, 1 - slot, c, top)
@@ -203,7 +209,7 @@
         return jnp.max(top, axis=0, keepdims=True)
 
     top = low()
-    q_first = of_head(0)
+    q_first = of_step(0)
     for c in range(keys // chunk):
         top = score(q_first, 0, c, top)
     peak = jnp.max(top, axis=0, keepdims=True)
@@ -212,14 +218,19 @@
         peak = step(2 * i, 0, peak, True)
         return step(2 * i + 1, 1, peak, True)
 
-    peak = lax.fori_loop(0, heads // 2 - 1, pair, peak)
-    peak = step(heads - 2, 0, peak, True)
-    step(heads - 1, 1, peak, False)
+    peak = lax.fori_loop(0, steps // 2 - 1, pair, peak)
+    peak = step(steps - 2, 0, peak, True)
+    step(steps - 1, 1, peak, False)
 
 
 def divide(at_ref):
-    def finish(head, peak, mixed):
-        at_ref[head] = (mixed[:HEAD] / mixed[HEAD:]).astype(bf16)
+    n = at_ref.shape[2]
+
+    def finish(step, peak, mixed):
+        for i in range(TOGETHER):
+            part = mixed[i * HEAD : (i + 1) * HEAD, i * n : (i + 1) * n]
+            total = mixed[TOGETHER * HEAD :, i * n : (i + 1) * n]
+            at_ref[step * TOGETHER + i] = (part / total).astype(bf16)
 
     return finish
 
@@ -233,15 +244,16 @@
     width = heads * HEAD
     return [
         pltpu.VMEM((keys, width), bf16),
-        pltpu.VMEM((heads, 2 * HEAD, keys), bf16),
-        pltpu.VMEM((2, keys, queries), f32),
+        pltpu.VMEM((heads // TOGETHER, SUMS, keys), bf16),
+        pltpu.VMEM((2, keys, TOGETHER * queries), f32),
     ]
 
 
 def load_values(vt_ref, values, heads):
     keys = values.shape[1]
-    vt_ref[:, :HEAD, :] = values.reshape(heads, HEAD, keys)
-    vt_ref[:, HEAD:, :] = jnp.ones((heads, HEAD, keys), bf16)
+    own = TOGETHER * HEAD
+    vt_ref[:, :own, :] = values.reshape(heads // TOGETHER, own, keys)
+    vt_ref[:, own:, :] = jnp.ones((heads // TOGETHER, HEAD, keys), bf16)
 
 
 SCALE = 1.0 / math.sqrt(HEAD)
@@ -504,8 +516,8 @@
         "attend4_own",
         [
             shape((C4, n)),
-            shape((H4, 1, n), f32),
-            shape((H4, 2 * HEAD, n), f32),
+            shape((H4 // TOGETHER, 1, TOGETHER * n), f32),
+            shape((H4 // TOGETHER, SUMS, TOGETHER * n), f32),
             shape((1, C5), f32),
         ],
         attend_scratch(H4, n, n),

time: 157 us -> 157 us (level)
  transfers between devices with their start and end apart: 3 -> 3, of which waited for: 2 -> 2; matrix products, arithmetic and copies ran while one was open for 0% -> 0% of each run, Pallas kernels for 5% -> 4%
where the time goes in v5:
time: 157 us
  blocking collectives  81.9 us (52%)
  starting transfers between devices  28.5 us (18%)
  Pallas kernels  24.3 us (15%)
  waiting for transfers between devices  18.8 us (12%)
  local copies, waits for them, and re-layouts  1.89 us (1%)
    all_to_all x5, blocking collectives, exchange(): return lax.all_to_all(block, axes, split_axis=0, concat_axis=0, tiled=True)  71.4 us
    all_to_all x2, starting transfers between devices, exchange(): return lax.all_to_all(block, axes, split_axis=0, concat_axis=0, tiled=True)  25.2 us
    all_to_all x2, waiting for transfers between devices, exchange(): return lax.all_to_all(block, axes, split_axis=0, concat_axis=0, tiled=True)  18.8 us
    pallas_call x1, Pallas kernels, local(): kernel(other_kernel, 'attend4_other', [shape((n, C4)), shape((nx, room +...  6.67 us
    pallas_call x1, Pallas kernels, local(): kernel(coarse_kernel, 'attend5', shape((nx, n, width)), attend_scratch(wi...  5.68 us
    pallas_call x1, Pallas kernels, local(): kernel(own_kernel, 'attend4_own', [shape((C4, n)), shape((H4 // TOGETHER,...  5.27 us
    all_gather x1, blocking collectives, local(): asked_both = lax.all_gather(asked, 'c', axis=0, tiled=True)  4.97 us
    ppermute x1, starting transfers between devices, local(): other4 = lax.ppermute(normed4, 'x', [(i, i ^ 1) for i in range(nx)])  3.29 us
  transfers between devices with their start and end apart: 3, of which 2 were waited for; matrix products, arithmetic and copies ran while one was open for 0% of the time, Pallas kernels for 4%

profile of v5, /device:TPU:1, one launch (start us, length us, event | category | flops | bytes accessed | tf_op | source)
XLA Modules:
  0.0 156.9 jit_solution(10697698382099929968)
XLA Ops:
  0.6 0.7 pad_add_fusion.orders_ref
  1.3 1.3 request.1
  2.6 15.9 %all-to-all-start = ((s32[16,4,16]{2,1,0:T(4,128)}), s32[16,4,16]{2,1,0:T(4,128)S(1)}, u32[]{:S(2)}, u32[]{:S(2)}) async-start(s32[16,4,16]{2,1,0:T(4,128)} %get-tuple-element.26), calls=%async_computation | async-start | bytes 65536 | tf_op jit(solution)/shard_map/all_to_all | solution.py:448
  18.5 3.0 %all_gather.9.table_ref = bf16[1024,256]{1,0:T(8,128)(2,1)S(1)} all-gather(bf16[512,256]{1,0:T(8,128)(2,1)} %param.12), channel_id=1, replica_groups=mesh['z'=16,'y'=4,'c'=2,'x'=4] {'c'}, dimensions={0}, use_global_device_ids=true | all-gather | bytes 786432 | tf_op jit(solution)/shard_map/all_gather | solution.py:478
  21.5 8.5 %all-to-all-done = s32[16,4,16]{2,1,0:T(4,128)S(1)} async-done(((s32[16,4,16]{2,1,0:T(4,128)}), s32[16,4,16]{2,1,0:T(4,128)S(1)}, u32[]{:S(2)}, u32[]{:S(2)}) %all-to-all-start) | async-done | bytes 4128 | tf_op jit(solution)/shard_map/all_to_all | solution.py:448
  30.0 0.1 copy.15
  30.0 0.1 all_to_all.26
  30.1 13.0 %all_to_all.41 = s32[16,1,64]{2,1,0:T(1,128)S(1)} all-to-all(s32[16,1,64]{2,1,0:T(1,128)S(1)} %bitcast.31), channel_id=1, replica_groups=mesh['z'=16,'y'=4,'c'=2,'x'=4] {'y','x'}, dimensions={0} | all-to-all | bytes 8192 | tf_op jit(solution)/shard_map/all_to_all | solution.py:448
  43.1 0.4 pick4.1
  43.5 0.8 reshape.30
  44.2 9.3 %all-to-all-start.2 = ((bf16[256,4,128]{2,1,0:T(4,128)(2,1)}), bf16[256,4,128]{2,1,0:T(4,128)(2,1)S(1)}, u32[]{:S(2)}, u32[]{:S(2)}) async-start(bf16[256,4,128]{2,1,0:T(4,128)(2,1)} %reshape.30), calls=%async_computation.2 | async-start | bytes 524288 | tf_op jit(solution)/shard_map/all_to_all | solution.py:448
  53.5 5.0 %all-gather = s32[32,1,64]{2,0,1:T(8,128)S(1)} all-gather(s32[16,1,64]{2,0,1:T(8,128)S(1)} %bitcast.22), channel_id=2, replica_groups=mesh['z'=16,'y'=4,'c'=2,'x'=4] {'c'}, dimensions={0}, use_global_device_ids=true | all-gather | bytes 12288 | tf_op jit(solution)/shard_map/all_gather | solution.py:487
  58.5 1.7 %prepare.1 = (bf16[512,512]{1,0:T(8,128)(2,1)S(1)}, bf16[512,512]{1,0:T(8,128)(2,1)S(1)}, bf16[512,1344]{1,0:T(8,128)(2,1)S(1)}, bf16[336,512]{1,0:T(8,128)(2,1)...) custom-call(s32[1,512]{1,0:T(1,128)S(1)} %get-tuple-element.24.owner_ref, ...), custom_call_target="tpu_custom_call" | custom-call | flops 268435456 | tf_op jit(solution)/shard_map/prepare/pallas_call | solution.py:497
  60.2 0.9 copy-done.8
  61.1 10.3 %all-to-all-done.2 = bf16[256,4,128]{2,1,0:T(4,128)(2,1)S(1)} async-done(((bf16[256,4,128]{2,1,0:T(4,128)(2,1)}), bf16[256,4,128]{2,1,0:T(4,128)(2,1)S(1)}, u32[]{:S(2)}, u32[]{:S(2)}) %all-to-all-start.2) | async-done | bytes 262176 | tf_op jit(solution)/shard_map/all_to_all | solution.py:448
  71.4 0.5 norm4.1
  71.9 3.3 %collective-permute-start = (bf16[512,256]{1,0:T(8,128)(2,1)S(1)}, bf16[512,256]{1,0:T(8,128)(2,1)S(1)}, u32[]{:S(2)}, u32[]{:S(2)}) collective-permute-start(bf16[512,256]{1,0:T(8,128)(2,1)S(1)} %get-tuple-element.31.own_ref), channel_id=1, source_target_pairs={{0,1},{1,0},{2,3},{3,2},{4,5},{5,4},{6,7},{7,6},{8,9},{9,8},{10,11... | collective-permute-start | bytes 786440 | tf_op jit(solution)/shard_map/ppermute | solution.py:512
  75.2 0.0 copy-start.4
  75.2 0.0 copy-start.5
  75.3 5.3 %attend4_own.1 = (bf16[256,512]{1,0:T(8,128)(2,1)S(1)}, f32[8,1,1024]{2,1,0:T(1,128)S(1)}, f32[8,48,1024]{2,1,0:T(8,128)S(1)}, f32[1,512]{1,0:T(1,128)S(1)}) custom-call(bf16[512,256]{1,0:T(8,128)(2,1)S(1)} %get-tuple-element.31.own_ref, bf16[3,256,256]{2,1,0:T(8,128)(2,1)S(1)} %copy-done.3, f32[1,512]{1,0:T(1,128)S(1)} %bitcast.27), custom_call_target="tpu_custom_call" | custom-call | flops 4294967296 | tf_op jit(solution)/shard_map/attend4_own/pallas_call | solution.py:514
  80.6 6.7 %attend4_other.1 = (bf16[512,256]{1,0:T(8,128)(2,1)}, bf16[4,352,128]{2,1,0:T(8,128)(2,1)S(1)}) custom-call(bf16[512,256]{1,0:T(8,128)(2,1)S(1)} %collective-permute-done.other_ref, bf16[3,256,256]{2,1,0:T(8,128)(2,1)S(1)} %copy-done.3, bf16[256,512]{1,0:T(8,128)(2,1)S(1)} %get-tuple-element.32.qt_ref, f32[8,1,1024]{2,1,0:T(1,128)S(1)} %get-tuple-element.33.peak_ref, ...), custom_call_target="tpu_custom_call" | custom-call | flops 4294967296 | tf_op jit(solution)/shard_map/attend4_other/pallas_call | solution.py:526
  87.3 9.2 %all_to_all.42.parts_ref = bf16[4,352,128]{2,1,0:T(8,128)(2,1)S(1)} all-to-all(bf16[4,352,128]{2,1,0:T(8,128)(2,1)S(1)} %get-tuple-element.40), channel_id=1, replica_groups=mesh['z'=16,'y'=4,'c'=2,'x'=4] {'x'}, dimensions={0} | all-to-all | bytes 720896 | tf_op jit(solution)/shard_map/all_to_all | solution.py:448
  96.5 0.7 pool.1
  97.1 0.0 copy-start
  97.2 16.3 %all_to_all.43.rows_ref = bf16[16,32,128]{2,1,0:T(8,128)(2,1)S(1)} all-to-all(bf16[16,32,128]{2,1,0:T(8,128)(2,1)S(1)} %bitcast.19), channel_id=1, replica_groups=mesh['z'=16,'y'=4,'c'=2,'x'=4] {'z'}, dimensions={0} | all-to-all | bytes 262144 | tf_op jit(solution)/shard_map/all_to_all | solution.py:448
  113.5 0.3 spread.1
  113.8 21.3 %all_to_all.44 = bf16[32,64,128]{2,1,0:T(8,128)(2,1)S(1)} all-to-all(bf16[32,64,128]{2,1,0:T(8,128)(2,1)S(1)} %bitcast.18), channel_id=1, replica_groups=mesh['z'=16,'y'=4,'c'=2,'x'=4] {'y','c','x'}, dimensions={0} | all-to-all | bytes 1048576 | tf_op jit(solution)/shard_map/all_to_all | solution.py:448
  135.1 1.1 norm5.1
  136.3 2.6 %all_gather.11.both_ref = bf16[1024,256]{1,0:T(8,128)(2,1)S(1)} all-gather(bf16[512,256]{1,0:T(8,128)(2,1)S(1)} %get-tuple-element.45), channel_id=1, replica_groups=mesh['z'=16,'y'=4,'c'=2,'x'=4] {'c'}, dimensions={0}, use_global_device_ids=true | all-gather | bytes 786432 | tf_op jit(solution)/shard_map/all_gather | solution.py:550
  138.9 5.7 %attend5.1 = bf16[4,512,128]{2,1,0:T(8,128)(2,1)S(1)} custom-call(bf16[512,128]{1,0:T(8,128)(2,1)S(1)} %get-tuple-element.44.q_ref, bf16[1024,256]{1,0:T(8,128)(2,1)S(1)} %all_gather.11.both_ref, bf16[128,512]{1,0:T(8,128)(2,1)S(1)} %copy-done.1), custom_call_target="tpu_custom_call" | custom-call | flops 268435456 | tf_op jit(solution)/shard_map/attend5/pallas_call | solution.py:551
  144.6 11.6 %all_to_all.45.parts_ref = bf16[4,512,128]{2,1,0:T(8,128)(2,1)S(1)} all-to-all(bf16[4,512,128]{2,1,0:T(8,128)(2,1)S(1)} %attend5.1), channel_id=1, replica_groups=mesh['z'=16,'y'=4,'c'=2,'x'=4] {'x'}, dimensions={0} | all-to-all | bytes 1048576 | tf_op jit(solution)/shard_map/all_to_all | solution.py:448
  156.2 0.7 add5.1
  (18 shorter events, 0.1 us)
Async XLA Ops:
  2.6 55.9 %copy-start.2 = (s32[512,8]{0,1:T(8,128)S(1)}, s32[512,8]{0,1:T(8,128)}, u32[]{:S(2)}) copy-start(s32[512,8]{0,1:T(8,128)} %param.18) | copy-start | bytes 49156
  2.6 55.9 %copy-start.7 = (f32[256]{0:T(256)S(1)}, f32[256]{0:T(256)}, u32[]{:S(2)}) copy-start(f32[256]{0:T(256)} %param.14) | copy-start | bytes 3076
  2.6 27.4 %all-to-all-start = ((s32[16,4,16]{2,1,0:T(4,128)}), s32[16,4,16]{2,1,0:T(4,128)S(1)}, u32[]{:S(2)}, u32[]{:S(2)}) async-start(s32[16,4,16]{2,1,0:T(4,128)} %get-tuple-element.26), calls=%async_computation | async-start | bytes 65536 | tf_op jit(solution)/shard_map/all_to_all | solution.py:448
  44.2 31.0 %copy-start.3 = (bf16[3,256,256]{2,1,0:T(8,128)(2,1)S(1)}, bf16[3,256,256]{2,1,0:T(8,128)(2,1)}, u32[]{:S(2)}) copy-start(bf16[3,256,256]{2,1,0:T(8,128)(2,1)} %qkv_ref.4) | copy-start | bytes 1179652
  44.2 31.0 %copy-start.6 = (f32[512]{0:T(512)S(1)}, f32[512]{0:T(512)}, u32[]{:S(2)}) copy-start(f32[512]{0:T(512)} %param.20) | copy-start | bytes 6148
  44.2 27.2 %all-to-all-start.2 = ((bf16[256,4,128]{2,1,0:T(4,128)(2,1)}), bf16[256,4,128]{2,1,0:T(4,128)(2,1)S(1)}, u32[]{:S(2)}, u32[]{:S(2)}) async-start(bf16[256,4,128]{2,1,0:T(4,128)(2,1)} %reshape.30), calls=%async_computation.2 | async-start | bytes 524288 | tf_op jit(solution)/shard_map/all_to_all | solution.py:448
  60.2 0.9 copy-start.8
  71.9 8.6 %collective-permute-start = (bf16[512,256]{1,0:T(8,128)(2,1)S(1)}, bf16[512,256]{1,0:T(8,128)(2,1)S(1)}, u32[]{:S(2)}, u32[]{:S(2)}) collective-permute-start(bf16[512,256]{1,0:T(8,128)(2,1)S(1)} %get-tuple-element.31.own_ref), channel_id=1, source_target_pairs={{0,1},{1,0},{2,3},{3,2},{4,5},{5,4},{6,7},{7,6},{8,9},{9,8},{10,11... | collective-permute-start | bytes 786440 | tf_op jit(solution)/shard_map/ppermute | solution.py:512
  75.2 5.3 %copy-start.4 = (bf16[256,512]{1,0:T(8,128)(2,1)S(1)}, bf16[256,512]{1,0:T(8,128)(2,1)}, u32[]{:S(2)}) copy-start(bf16[256,512]{1,0:T(8,128)(2,1)} %weight_ref.1) | copy-start | bytes 786436
  75.2 5.3 %copy-start.5 = (bf16[256,256]{1,0:T(8,128)(2,1)S(1)}, bf16[256,256]{1,0:T(8,128)(2,1)}, u32[]{:S(2)}) copy-start(bf16[256,256]{1,0:T(8,128)(2,1)} %proj_ref.2) | copy-start | bytes 393220
  75.3 5.3 %copy-start.9 = (f32[3,512,128]{2,1,0:T(8,128)S(1)}, f32[3,512,128]{2,1,0:T(8,128)}, u32[]{:S(2)}) copy-start(f32[3,512,128]{2,1,0:T(8,128)} %copy-done.8) | copy-start | bytes 2359300
  97.1 38.0 %copy-start = (bf16[3,512,128]{2,1,0:T(8,128)(2,1)S(1)}, bf16[3,512,128]{2,1,0:T(8,128)(2,1)}, u32[]{:S(2)}) copy-start(bf16[3,512,128]{2,1,0:T(8,128)(2,1)} %qkv_ref.5) | copy-start | bytes 1179652
  113.8 25.1 %copy-start.1 = (bf16[128,512]{1,0:T(8,128)(2,1)S(1)}, bf16[128,512]{1,0:T(8,128)(2,1)}, u32[]{:S(2)}) copy-start(bf16[128,512]{1,0:T(8,128)(2,1)} %proj_ref.3) | copy-start | bytes 393220

commit v6 on v5

--- a/solution.py
+++ b/solution.py
@@ -172,15 +172,16 @@
 
 
 def attend(heads, k_ref, qt_ref, vt_ref, s_ref, finish, before=None, chunk=512):
-    steps = heads // TOGETHER
     queries = s_ref.shape[2]
+    together = queries // qt_ref.shape[1]
+    steps = heads // together
     keys = k_ref.shape[0]
     row_head = lax.broadcasted_iota(jnp.int32, qt_ref.shape, 0) // HEAD
 
     def of_step(step):
         q = qt_ref[...]
         none = jnp.zeros_like(q)
-        each = [jnp.where(row_head == step * TOGETHER + i, q, none) for i in range(TOGETHER)]
+        each = [jnp.where(row_head == step * together + i, q, none) for i in range(together)]
         return jnp.concatenate(each, axis=1)
 
     def score(q_head, slot, c, top):
@@ -193,7 +194,7 @@
 
     def step(head, slot, peak, more):
         if before is None:
-            mixed = jnp.zeros((SUMS, queries), f32)
+            mixed = jnp.zeros((vt_ref.shape[1], queries), f32)
         else:
             earlier, mixed = before(head)
             peak = jnp.maximum(peak, earlier)
@@ -227,10 +228,11 @@
     n = at_ref.shape[2]
 
     def finish(step, peak, mixed):
-        for i in range(TOGETHER):
+        together = mixed.shape[1] // n
+        for i in range(together):
             part = mixed[i * HEAD : (i + 1) * HEAD, i * n : (i + 1) * n]
-            total = mixed[TOGETHER * HEAD :, i * n : (i + 1) * n]
-            at_ref[step * TOGETHER + i] = (part / total).astype(bf16)
+            total = mixed[together * HEAD :, i * n : (i + 1) * n]
+            at_ref[step * together + i] = (part / total).astype(bf16)
 
     return finish
 
@@ -240,20 +242,20 @@
     return jnp.transpose(at_ref[...].reshape(heads * size, queries))
 
 
-def attend_scratch(heads, queries, keys):
+def attend_scratch(heads, queries, keys, together):
     width = heads * HEAD
     return [
         pltpu.VMEM((keys, width), bf16),
-        pltpu.VMEM((heads // TOGETHER, SUMS, keys), bf16),
-        pltpu.VMEM((2, keys, TOGETHER * queries), f32),
+        pltpu.VMEM((heads // together, (together + 1) * HEAD, keys), bf16),
+        pltpu.VMEM((2, keys, together * queries), f32),
     ]
 
 
 def load_values(vt_ref, values, heads):
     keys = values.shape[1]
-    own = TOGETHER * HEAD
-    vt_ref[:, :own, :] = values.reshape(heads // TOGETHER, own, keys)
-    vt_ref[:, own:, :] = jnp.ones((heads // TOGETHER, HEAD, keys), bf16)
+    own = vt_ref.shape[1] - HEAD
+    vt_ref[:, :own, :] = values.reshape(vt_ref.shape[0], own, keys)
+    vt_ref[:, own:, :] = jnp.ones((vt_ref.shape[0], HEAD, keys), bf16)
 
 
 SCALE = 1.0 / math.sqrt(HEAD)
@@ -520,14 +522,14 @@
             shape((H4 // TOGETHER, SUMS, TOGETHER * n), f32),
             shape((1, C5), f32),
         ],
-        attend_scratch(H4, n, n),
+        attend_scratch(H4, n, n, TOGETHER),
         flops=half,
     )(normed4, qkv4, gain5.reshape(1, C5))
     fine_out, parts4 = kernel(
         other_kernel,
         "attend4_other",
         [shape((n, C4)), shape((nx, room + EDGE, width))],
-        attend_scratch(H4, n, n)
+        attend_scratch(H4, n, n, TOGETHER)
         + [pltpu.VMEM((H4, HEAD, n), bf16), pltpu.VMEM((n, C4), bf16), DMA((1,))],
         flops=half,
         out_specs=[pl.BlockSpec(memory_space=pl.ANY), VMEM],
@@ -552,7 +554,7 @@
         coarse_kernel,
         "attend5",
         shape((nx, n, width)),
-        attend_scratch(width // HEAD, n, 2 * n)
+        attend_scratch(width // HEAD, n, 2 * n, 1)
         + [pltpu.VMEM((width, n), bf16), pltpu.VMEM((width // HEAD, HEAD, n), bf16)],
     )(query5, both5, proj5)
     coarse_out = kernel(sum_kernel, "add5", shape((n, width)))(own_columns, exchange(terms, "x"))

time: 157 us -> 157 us (level)
  no operation moved by 1% of the time
where the time goes in v6:
time: 157 us; the launch traced here: 156 us
  blocking collectives  81.7 us (52%)
  starting transfers between devices  28.5 us (18%)
  Pallas kernels  23.7 us (15%)
  waiting for transfers between devices  18.8 us (12%)
  local copies, waits for them, and re-layouts  1.89 us (1%)
    all_to_all x5, blocking collectives, exchange(): return lax.all_to_all(block, axes, split_axis=0, concat_axis=0, tiled=True)  71.4 us
    all_to_all x2, starting transfers between devices, exchange(): return lax.all_to_all(block, axes, split_axis=0, concat_axis=0, tiled=True)  25.2 us
    all_to_all x2, waiting for transfers between devices, exchange(): return lax.all_to_all(block, axes, split_axis=0, concat_axis=0, tiled=True)  18.8 us
    pallas_call x1, Pallas kernels, local(): kernel(other_kernel, 'attend4_other', [shape((n, C4)), shape((nx, room +...  6.67 us
    pallas_call x1, Pallas kernels, local(): kernel(own_kernel, 'attend4_own', [shape((C4, n)), shape((H4 // TOGETHER,...  5.27 us
    pallas_call x1, Pallas kernels, local(): kernel(coarse_kernel, 'attend5', shape((nx, n, width)), attend_scratch(wi...  5.06 us
    all_gather x1, blocking collectives, local(): asked_both = lax.all_gather(asked, 'c', axis=0, tiled=True)  4.97 us
    ppermute x1, starting transfers between devices, local(): other4 = lax.ppermute(normed4, 'x', [(i, i ^ 1) for i in range(nx)])  3.29 us
  transfers between devices with their start and end apart: 3, of which 2 were waited for; matrix products, arithmetic and copies ran while one was open for 0% of the time, Pallas kernels for 4%

profile of v6, /device:TPU:1, one launch (start us, length us, event | category | flops | bytes accessed | tf_op | source)
XLA Modules:
  0.0 156.0 jit_solution(7567005837316150607)
XLA Ops:
  0.6 0.7 pad_add_fusion.orders_ref
  1.3 1.3 request.1
  2.6 15.9 %all-to-all-start = ((s32[16,4,16]{2,1,0:T(4,128)}), s32[16,4,16]{2,1,0:T(4,128)S(1)}, u32[]{:S(2)}, u32[]{:S(2)}) async-start(s32[16,4,16]{2,1,0:T(4,128)} %get-tuple-element.26), calls=%async_computation | async-start | bytes 65536 | tf_op jit(solution)/shard_map/all_to_all | solution.py:450
  18.5 3.0 %all_gather.9.table_ref = bf16[1024,256]{1,0:T(8,128)(2,1)S(1)} all-gather(bf16[512,256]{1,0:T(8,128)(2,1)} %param.12), channel_id=1, replica_groups=mesh['z'=16,'y'=4,'c'=2,'x'=4] {'c'}, dimensions={0}, use_global_device_ids=true | all-gather | bytes 786432 | tf_op jit(solution)/shard_map/all_gather | solution.py:480
  21.5 8.5 %all-to-all-done = s32[16,4,16]{2,1,0:T(4,128)S(1)} async-done(((s32[16,4,16]{2,1,0:T(4,128)}), s32[16,4,16]{2,1,0:T(4,128)S(1)}, u32[]{:S(2)}, u32[]{:S(2)}) %all-to-all-start) | async-done | bytes 4128 | tf_op jit(solution)/shard_map/all_to_all | solution.py:450
  30.0 0.1 copy.15
  30.0 0.1 all_to_all.26
  30.1 13.0 %all_to_all.41 = s32[16,1,64]{2,1,0:T(1,128)S(1)} all-to-all(s32[16,1,64]{2,1,0:T(1,128)S(1)} %bitcast.31), channel_id=1, replica_groups=mesh['z'=16,'y'=4,'c'=2,'x'=4] {'y','x'}, dimensions={0} | all-to-all | bytes 8192 | tf_op jit(solution)/shard_map/all_to_all | solution.py:450
  43.1 0.4 pick4.1
  43.5 0.8 reshape.30
  44.2 9.3 %all-to-all-start.2 = ((bf16[256,4,128]{2,1,0:T(4,128)(2,1)}), bf16[256,4,128]{2,1,0:T(4,128)(2,1)S(1)}, u32[]{:S(2)}, u32[]{:S(2)}) async-start(bf16[256,4,128]{2,1,0:T(4,128)(2,1)} %reshape.30), calls=%async_computation.2 | async-start | bytes 524288 | tf_op jit(solution)/shard_map/all_to_all | solution.py:450
  53.5 5.0 %all-gather = s32[32,1,64]{2,0,1:T(8,128)S(1)} all-gather(s32[16,1,64]{2,0,1:T(8,128)S(1)} %bitcast.22), channel_id=2, replica_groups=mesh['z'=16,'y'=4,'c'=2,'x'=4] {'c'}, dimensions={0}, use_global_device_ids=true | all-gather | bytes 12288 | tf_op jit(solution)/shard_map/all_gather | solution.py:489
  58.5 1.7 %prepare.1 = (bf16[512,512]{1,0:T(8,128)(2,1)S(1)}, bf16[512,512]{1,0:T(8,128)(2,1)S(1)}, bf16[512,1344]{1,0:T(8,128)(2,1)S(1)}, bf16[336,512]{1,0:T(8,128)(2,1)...) custom-call(s32[1,512]{1,0:T(1,128)S(1)} %get-tuple-element.24.owner_ref, ...), custom_call_target="tpu_custom_call" | custom-call | flops 268435456 | tf_op jit(solution)/shard_map/prepare/pallas_call | solution.py:499
  60.2 0.9 copy-done.8
  61.1 10.3 %all-to-all-done.2 = bf16[256,4,128]{2,1,0:T(4,128)(2,1)S(1)} async-done(((bf16[256,4,128]{2,1,0:T(4,128)(2,1)}), bf16[256,4,128]{2,1,0:T(4,128)(2,1)S(1)}, u32[]{:S(2)}, u32[]{:S(2)}) %all-to-all-start.2) | async-done | bytes 262176 | tf_op jit(solution)/shard_map/all_to_all | solution.py:450
  71.4 0.5 norm4.1
  71.9 3.3 %collective-permute-start = (bf16[512,256]{1,0:T(8,128)(2,1)S(1)}, bf16[512,256]{1,0:T(8,128)(2,1)S(1)}, u32[]{:S(2)}, u32[]{:S(2)}) collective-permute-start(bf16[512,256]{1,0:T(8,128)(2,1)S(1)} %get-tuple-element.31.own_ref), channel_id=1, source_target_pairs={{0,1},{1,0},{2,3},{3,2},{4,5},{5,4},{6,7},{7,6},{8,9},{9,8},{10,11... | collective-permute-start | bytes 786440 | tf_op jit(solution)/shard_map/ppermute | solution.py:514
  75.2 0.0 copy-start.4
  75.2 0.0 copy-start.5
  75.3 5.3 %attend4_own.1 = (bf16[256,512]{1,0:T(8,128)(2,1)S(1)}, f32[8,1,1024]{2,1,0:T(1,128)S(1)}, f32[8,48,1024]{2,1,0:T(8,128)S(1)}, f32[1,512]{1,0:T(1,128)S(1)}) custom-call(bf16[512,256]{1,0:T(8,128)(2,1)S(1)} %get-tuple-element.31.own_ref, bf16[3,256,256]{2,1,0:T(8,128)(2,1)S(1)} %copy-done.3, f32[1,512]{1,0:T(1,128)S(1)} %bitcast.27), custom_call_target="tpu_custom_call" | custom-call | flops 4294967296 | tf_op jit(solution)/shard_map/attend4_own/pallas_call | solution.py:516
  80.6 6.7 %attend4_other.1 = (bf16[512,256]{1,0:T(8,128)(2,1)}, bf16[4,352,128]{2,1,0:T(8,128)(2,1)S(1)}) custom-call(bf16[512,256]{1,0:T(8,128)(2,1)S(1)} %collective-permute-done.other_ref, bf16[3,256,256]{2,1,0:T(8,128)(2,1)S(1)} %copy-done.3, bf16[256,512]{1,0:T(8,128)(2,1)S(1)} %get-tuple-element.32.qt_ref, f32[8,1,1024]{2,1,0:T(1,128)S(1)} %get-tuple-element.33.peak_ref, ...), custom_call_target="tpu_custom_call" | custom-call | flops 4294967296 | tf_op jit(solution)/shard_map/attend4_other/pallas_call | solution.py:528
  87.3 9.2 %all_to_all.42.parts_ref = bf16[4,352,128]{2,1,0:T(8,128)(2,1)S(1)} all-to-all(bf16[4,352,128]{2,1,0:T(8,128)(2,1)S(1)} %get-tuple-element.40), channel_id=1, replica_groups=mesh['z'=16,'y'=4,'c'=2,'x'=4] {'x'}, dimensions={0} | all-to-all | bytes 720896 | tf_op jit(solution)/shard_map/all_to_all | solution.py:450
  96.5 0.7 pool.1
  97.2 16.3 %all_to_all.43.rows_ref = bf16[16,32,128]{2,1,0:T(8,128)(2,1)S(1)} all-to-all(bf16[16,32,128]{2,1,0:T(8,128)(2,1)S(1)} %bitcast.19), channel_id=1, replica_groups=mesh['z'=16,'y'=4,'c'=2,'x'=4] {'z'}, dimensions={0} | all-to-all | bytes 262144 | tf_op jit(solution)/shard_map/all_to_all | solution.py:450
  113.5 0.3 spread.1
  113.8 0.0 copy-start.1
  113.8 21.3 %all_to_all.44 = bf16[32,64,128]{2,1,0:T(8,128)(2,1)S(1)} all-to-all(bf16[32,64,128]{2,1,0:T(8,128)(2,1)S(1)} %bitcast.18), channel_id=1, replica_groups=mesh['z'=16,'y'=4,'c'=2,'x'=4] {'y','c','x'}, dimensions={0} | all-to-all | bytes 1048576 | tf_op jit(solution)/shard_map/all_to_all | solution.py:450
  135.1 1.1 norm5.1
  136.3 2.4 %all_gather.11.both_ref = bf16[1024,256]{1,0:T(8,128)(2,1)S(1)} all-gather(bf16[512,256]{1,0:T(8,128)(2,1)S(1)} %get-tuple-element.45), channel_id=1, replica_groups=mesh['z'=16,'y'=4,'c'=2,'x'=4] {'c'}, dimensions={0}, use_global_device_ids=true | all-gather | bytes 786432 | tf_op jit(solution)/shard_map/all_gather | solution.py:552
  138.6 5.1 %attend5.1 = bf16[4,512,128]{2,1,0:T(8,128)(2,1)S(1)} custom-call(bf16[512,128]{1,0:T(8,128)(2,1)S(1)} %get-tuple-element.44.q_ref, bf16[1024,256]{1,0:T(8,128)(2,1)S(1)} %all_gather.11.both_ref, bf16[128,512]{1,0:T(8,128)(2,1)S(1)} %copy-done.1), custom_call_target="tpu_custom_call" | custom-call | flops 268435456 | tf_op jit(solution)/shard_map/attend5/pallas_call | solution.py:553
  143.7 11.6 %all_to_all.45.parts_ref = bf16[4,512,128]{2,1,0:T(8,128)(2,1)S(1)} all-to-all(bf16[4,512,128]{2,1,0:T(8,128)(2,1)S(1)} %attend5.1), channel_id=1, replica_groups=mesh['z'=16,'y'=4,'c'=2,'x'=4] {'x'}, dimensions={0} | all-to-all | bytes 1048576 | tf_op jit(solution)/shard_map/all_to_all | solution.py:450
  155.3 0.7 add5.1
  (18 shorter events, 0.1 us)
Async XLA Ops:
  2.6 55.9 %copy-start.2 = (s32[512,8]{0,1:T(8,128)S(1)}, s32[512,8]{0,1:T(8,128)}, u32[]{:S(2)}) copy-start(s32[512,8]{0,1:T(8,128)} %param.18) | copy-start | bytes 49156
  2.6 55.9 %copy-start.7 = (f32[256]{0:T(256)S(1)}, f32[256]{0:T(256)}, u32[]{:S(2)}) copy-start(f32[256]{0:T(256)} %param.14) | copy-start | bytes 3076
  2.6 27.4 %all-to-all-start = ((s32[16,4,16]{2,1,0:T(4,128)}), s32[16,4,16]{2,1,0:T(4,128)S(1)}, u32[]{:S(2)}, u32[]{:S(2)}) async-start(s32[16,4,16]{2,1,0:T(4,128)} %get-tuple-element.26), calls=%async_computation | async-start | bytes 65536 | tf_op jit(solution)/shard_map/all_to_all | solution.py:450
  44.2 31.0 %copy-start.3 = (bf16[3,256,256]{2,1,0:T(8,128)(2,1)S(1)}, bf16[3,256,256]{2,1,0:T(8,128)(2,1)}, u32[]{:S(2)}) copy-start(bf16[3,256,256]{2,1,0:T(8,128)(2,1)} %qkv_ref.4) | copy-start | bytes 1179652
  44.2 31.0 %copy-start.6 = (f32[512]{0:T(512)S(1)}, f32[512]{0:T(512)}, u32[]{:S(2)}) copy-start(f32[512]{0:T(512)} %param.20) | copy-start | bytes 6148
  44.2 27.2 %all-to-all-start.2 = ((bf16[256,4,128]{2,1,0:T(4,128)(2,1)}), bf16[256,4,128]{2,1,0:T(4,128)(2,1)S(1)}, u32[]{:S(2)}, u32[]{:S(2)}) async-start(bf16[256,4,128]{2,1,0:T(4,128)(2,1)} %reshape.30), calls=%async_computation.2 | async-start | bytes 524288 | tf_op jit(solution)/shard_map/all_to_all | solution.py:450
  60.2 0.9 copy-start.8
  71.9 8.6 %collective-permute-start = (bf16[512,256]{1,0:T(8,128)(2,1)S(1)}, bf16[512,256]{1,0:T(8,128)(2,1)S(1)}, u32[]{:S(2)}, u32[]{:S(2)}) collective-permute-start(bf16[512,256]{1,0:T(8,128)(2,1)S(1)} %get-tuple-element.31.own_ref), channel_id=1, source_target_pairs={{0,1},{1,0},{2,3},{3,2},{4,5},{5,4},{6,7},{7,6},{8,9},{9,8},{10,11... | collective-permute-start | bytes 786440 | tf_op jit(solution)/shard_map/ppermute | solution.py:514
  75.2 5.3 %copy-start.4 = (bf16[256,512]{1,0:T(8,128)(2,1)S(1)}, bf16[256,512]{1,0:T(8,128)(2,1)}, u32[]{:S(2)}) copy-start(bf16[256,512]{1,0:T(8,128)(2,1)} %weight_ref.1) | copy-start | bytes 786436
  75.2 5.3 %copy-start.5 = (bf16[256,256]{1,0:T(8,128)(2,1)S(1)}, bf16[256,256]{1,0:T(8,128)(2,1)}, u32[]{:S(2)}) copy-start(bf16[256,256]{1,0:T(8,128)(2,1)} %proj_ref.2) | copy-start | bytes 393220
  75.3 5.3 %copy-start.9 = (f32[3,512,128]{2,1,0:T(8,128)S(1)}, f32[3,512,128]{2,1,0:T(8,128)}, u32[]{:S(2)}) copy-start(f32[3,512,128]{2,1,0:T(8,128)} %copy-done.8) | copy-start | bytes 2359300
  97.1 38.0 %copy-start = (bf16[3,512,128]{2,1,0:T(8,128)(2,1)S(1)}, bf16[3,512,128]{2,1,0:T(8,128)(2,1)}, u32[]{:S(2)}) copy-start(bf16[3,512,128]{2,1,0:T(8,128)(2,1)} %qkv_ref.5) | copy-start | bytes 1179652
  113.8 24.9 %copy-start.1 = (bf16[128,512]{1,0:T(8,128)(2,1)S(1)}, bf16[128,512]{1,0:T(8,128)(2,1)}, u32[]{:S(2)}) copy-start(bf16[128,512]{1,0:T(8,128)(2,1)} %proj_ref.3) | copy-start | bytes 393220
